TPU v7x, 128 devices: a whole 4x4x4 slice. The times are simulated.
128 devices in a mesh: vocab: 4 (over z_lo, core), fsdp: 32 (over y, z_hi, x).
Axes of the slice: x: 4, y: 4, z: 4 (z_hi: 2, z_lo: 2; z = z_hi * 2 + z_lo), core: 2. Of those that a mesh axis runs over, the one named last changes fastest.
Arguments:
- hidden: bfloat16 [2, 1536, 4096], P(None, 'fsdp'), may hold values from -1000 to 1000
- norm_gain: bfloat16 [4096], replicated, may hold values from 0.5 to 1.5
- labels: int32 [2, 1536], P(None, 'fsdp'), may hold values from 0 to 65535
- head_weight: bfloat16 [4096, 65536], P(None, ('vocab', 'fsdp')), may hold values from -1 to 1
- head_ema: float32 [4096, 65536], P(None, ('vocab', 'fsdp')), may hold values from 1e-09 to 0.001
- gain_ema: float32 [4096], replicated, may hold values from 0.0001 to 0.03
Outputs:
- head_ema_new: float32 [4096, 65536], P(None, ('vocab', 'fsdp'))
- gain_ema_new: float32 [4096], replicated
All inputs are finite; a program needn't handle non-finite values.
Results may differ from a plain program's by a relative error of at most 0.00049.
Values may be sent and summed in bfloat16 or wider, within the bound.
No kernel may reach another device: no remote copies, remote signals or barrier semaphores. Data moves between devices by JAX's collectives and lax.ppermute only.
A program may use at most 192 MiB of HBM per device.

v0:
```python
import jax
import jax.numpy as jnp
from jax import lax
from jax.sharding import Mesh
from jax.sharding import PartitionSpec as P

VOCAB_FSDP = ("vocab_0", "vocab_1", "fsdp_0", "fsdp_1", "fsdp_2")
FSDP = ("fsdp_0", "fsdp_1", "fsdp_2")


BETA = 0.99
EPS = 1e-05


def gathered_once(value, axis):
    leaves = jax.tree.leaves(value)
    order = sorted(range(len(leaves)), key=lambda k: -leaves[k].size)
    width = (1, *leaves[order[0]].shape)[-1]
    lines = [
        jnp.pad(leaves[k].reshape(-1), (0, -leaves[k].size % width)).reshape(-1, width)
        for k in order
    ]
    both, at, found = (lax.all_gather(jnp.concatenate(lines), axis), 0, {})
    for k, line in zip(order, lines):
        section = both[:, at : at + len(line)].reshape(len(both), -1)
        found[k] = section[:, : leaves[k].size].reshape(-1, *leaves[k].shape)
        at += len(line)
    numbers = iter(range(len(leaves)))
    return jax.tree.map(lambda _: found[next(numbers)], value)


def combined_by_axis(value, axes, combine):
    for axis in axes:
        pieces = gathered_once(value, axis)
        value = jax.tree.map(lambda part: part[0], pieces)
        for k in range(1, lax.axis_size(axis)):
            value = combine(value, jax.tree.map(lambda part: part[k], pieces))
    return value


def combine_stats(earlier, later):
    first_top, first_total = earlier
    second_top, second_total = later
    joined_top = jnp.maximum(first_top, second_top)
    joined_total = first_total * jnp.exp(first_top - joined_top) + second_total * jnp.exp(
        second_top - joined_top
    )
    return (joined_top, joined_total)


def on_device(hidden, norm_gain, labels, head_weight, head_ema, gain_ema):
    batches, own_rows, features = hidden.shape
    columns = head_weight.shape[1]
    column_ids = lax.iota(jnp.int32, columns)[None, :] + lax.axis_index(VOCAB_FSDP) * columns
    gain_wide = norm_gain.astype(jnp.float32)
    wide = hidden.astype(jnp.float32)
    factor = lax.rsqrt(jnp.mean(wide * wide, axis=-1, keepdims=True) + EPS)
    scaled = (wide * factor * gain_wide).astype(jnp.bfloat16)
    count = batches * own_rows * lax.axis_size(FSDP)
    gradient = jnp.zeros((features, columns), jnp.float32)
    for batch in range(batches):
        batch_rows = scaled[batch]
        batch_labels = labels[batch]
        rows_all, labels_all = (
            lax.all_gather(batch_rows, FSDP, axis=0, tiled=True),
            lax.all_gather(batch_labels, FSDP, axis=0, tiled=True),
        )
        logits = jnp.dot(rows_all, head_weight, preferred_element_type=jnp.float32)
        local_top = jnp.max(logits, axis=1)
        local_total = jnp.sum(jnp.exp(logits - local_top[:, None]), axis=1)
        row_top, row_total = combined_by_axis((local_top, local_total), VOCAB_FSDP, combine_stats)
        chances = jnp.exp(logits - row_top[:, None]) / row_total[:, None]
        hits = (labels_all[:, None] == column_ids).astype(jnp.float32)
        slope = (chances - hits).astype(jnp.bfloat16)
        gradient = gradient + lax.dot_general(
            rows_all, slope, (((0,), (0,)), ((), ())), preferred_element_type=jnp.float32
        )
    head_new = BETA * head_ema + (1.0 - BETA) * gradient * gradient / count
    partial_sum = jnp.sum(head_weight.astype(jnp.float32) * gradient, axis=1)
    gain_grad = lax.psum(partial_sum, VOCAB_FSDP) / gain_wide
    gain_new = BETA * gain_ema + (1.0 - BETA) * gain_grad * gain_grad / count
    return (head_new, gain_new)


def solution(mesh):
    finer = Mesh(
        mesh.devices.reshape(2, 2, 4, 2, 4), ("vocab_0", "vocab_1", "fsdp_0", "fsdp_1", "fsdp_2")
    )
    return jax.shard_map(
        on_device,
        mesh=finer,
        in_specs=(
            P(None, FSDP, None),
            P(),
            P(None, FSDP),
            P(None, VOCAB_FSDP),
            P(None, VOCAB_FSDP),
            P(),
        ),
        out_specs=(P(None, VOCAB_FSDP), P()),
        check_vma=False,
    )
```

profile of v0, /device:TPU:6, one launch (start us, length us, event | category | flops | bytes accessed | tf_op | source)
XLA Modules:
  0.0 435.7 jit_solution(9790787997291281345)
XLA Ops:
  7.2 1.4 fusion.13
  8.6 0.7 convert_element_type.25
  9.3 1.4 fusion.15
  10.7 1.0 fusion.84
  11.7 0.7 all-gather.27.cloned.1.call-update
  12.4 6.4 %copy.12 = bf16[4096,512]{0,1:T(8,128)(2,1)} copy(bf16[4096,512]{1,0:T(8,128)(2,1)} %param.9) | data formatting | bytes 8388608 | tf_op args[3]
  18.9 9.0 %copy.11 = f32[4096,512]{0,1:T(8,128)} copy(f32[4096,512]{1,0:T(8,128)} %param.10) | data formatting | bytes 16777216 | tf_op args[4]
  27.9 0.6 dynamic-slice
  29.3 172.5 %all-reduce.2 = (s32[1536]{0:T(1024)S(1)}, s32[1536]{0:T(1024)S(1)}) all-reduce(s32[1536]{0:T(1024)S(1)} %bitcast_dynamic-update-slice_fusion, s32[1536]{0:T(1024)S(1)} %bitcast_dynamic-update-slice_fusion.1), channel_id=15, replica_groups=mesh['vocab_0'=2,'vocab_1'=2,'fsdp_0'=4,'fsdp_1'=2,'fsdp_2'=4] {'fsdp_0'..., use_global_device_ids=true, to_apply=%add.1 | all-reduce | flops 3072 | bytes 24576
  201.8 10.8 %fusion.85 = (f32[1536]{0:T(1024)S(1)}, f32[1536,512]{0,1:T(8,128)S(1)}) fusion(bf16[4096,512]{1,0:T(8,128)(2,1)} %param.9, bf16[1,1536,4096]{2,1,0:T(8,128)(2,1)} %all-gather.29.cloned.1.call-done), kind=kOutput, calls=%fused_computation.156 | convolution fusion | flops 6443235840 | bytes 19929088 | tf_op jit(solution)/shard_map/dot_general | solution.py:68
  212.7 1.7 copy-done.1
  214.4 0.5 exponential_reduce_fusion
  214.9 4.6 %all-gather.19 = f32[2,2,1536]{2,1,0:T(2,128)S(1)} all-gather(f32[1,2,1536]{2,1,0:T(2,128)S(1)} %maximum_bitcast_fusion.5), channel_id=10, replica_groups=mesh['vocab_0'=2,'vocab_1'=2,'fsdp_0'=4,'fsdp_1'=2,'fsdp_2'=4] {'vocab_0'}, dimensions={0}, use_global_device_ids=true | all-gather | bytes 36864 | tf_op jit(solution)/shard_map/all_gather | solution.py:23
  219.6 1.8 all-gather.20
  221.5 11.9 %all-gather.21 = f32[4,2,1536]{2,1,0:T(2,128)S(1)} all-gather(f32[1,2,1536]{2,1,0:T(2,128)S(1)} %maximum_bitcast_fusion.7), channel_id=12, replica_groups=mesh['vocab_0'=2,'vocab_1'=2,'fsdp_0'=4,'fsdp_1'=2,'fsdp_2'=4] {'fsdp_0'}, dimensions={0}, use_global_device_ids=true | all-gather | bytes 61440 | tf_op jit(solution)/shard_map/all_gather | solution.py:23
  233.5 12.6 %all-gather.22 = f32[2,2,1536]{2,1,0:T(2,128)S(1)} all-gather(f32[1,2,1536]{2,1,0:T(2,128)S(1)} %maximum_bitcast_fusion.8), channel_id=13, replica_groups=mesh['vocab_0'=2,'vocab_1'=2,'fsdp_0'=4,'fsdp_1'=2,'fsdp_2'=4] {'fsdp_1'}, dimensions={0}, use_global_device_ids=true | all-gather | bytes 36864 | tf_op jit(solution)/shard_map/all_gather | solution.py:23
  246.1 16.6 %all-gather.23 = f32[4,2,1536]{2,1,0:T(2,128)S(1)} all-gather(f32[1,2,1536]{2,1,0:T(2,128)S(1)} %maximum_bitcast_fusion.9), channel_id=14, replica_groups=mesh['vocab_0'=2,'vocab_1'=2,'fsdp_0'=4,'fsdp_1'=2,'fsdp_2'=4] {'fsdp_2'}, dimensions={0}, use_global_device_ids=true | all-gather | bytes 61440 | tf_op jit(solution)/shard_map/all_gather | solution.py:23
  262.7 0.1 slice_reduce_fusion.3
  262.8 13.8 %all-gather.27.cloned.1.call-done = bf16[1,1536,4096]{2,1,0:T(8,128)(2,1)} async-done(((bf16[1,48,4096]{2,1,0:T(8,128)(2,1)}), bf16[1,1536,4096]{2,1,0:T(8,128)(2,1)}) %all-gather.27.cloned.1.call-update) | async-done | bytes 12582928 | tf_op jit(solution)/shard_map/all_gather | solution.py:65
  276.7 10.7 %fusion.86 = (f32[1536]{0:T(1024)S(1)}, f32[1536,512]{0,1:T(8,128)S(1)}) fusion(bf16[4096,512]{1,0:T(8,128)(2,1)} %param.9, bf16[1,1536,4096]{2,1,0:T(8,128)(2,1)} %all-gather.27.cloned.1.call-done), kind=kOutput, calls=%fused_computation.157 | convolution fusion | flops 6443235840 | bytes 19929088 | tf_op jit(solution)/shard_map/dot_general | solution.py:68
  287.4 0.5 exponential_reduce_fusion.1
  287.9 4.5 %all-gather.14 = f32[2,2,1536]{2,1,0:T(2,128)S(1)} all-gather(f32[1,2,1536]{2,1,0:T(2,128)S(1)} %maximum_bitcast_fusion), channel_id=3, replica_groups=mesh['vocab_0'=2,'vocab_1'=2,'fsdp_0'=4,'fsdp_1'=2,'fsdp_2'=4] {'vocab_0'}, dimensions={0}, use_global_device_ids=true | all-gather | bytes 36864 | tf_op jit(solution)/shard_map/all_gather | solution.py:23
  292.5 1.8 all-gather.15
  294.3 11.9 %all-gather.16 = f32[4,2,1536]{2,1,0:T(2,128)S(1)} all-gather(f32[1,2,1536]{2,1,0:T(2,128)S(1)} %maximum_bitcast_fusion.2), channel_id=5, replica_groups=mesh['vocab_0'=2,'vocab_1'=2,'fsdp_0'=4,'fsdp_1'=2,'fsdp_2'=4] {'fsdp_0'}, dimensions={0}, use_global_device_ids=true | all-gather | bytes 61440 | tf_op jit(solution)/shard_map/all_gather | solution.py:23
  306.4 5.9 %all-gather.17 = f32[2,2,1536]{2,1,0:T(2,128)S(1)} all-gather(f32[1,2,1536]{2,1,0:T(2,128)S(1)} %maximum_bitcast_fusion.3), channel_id=6, replica_groups=mesh['vocab_0'=2,'vocab_1'=2,'fsdp_0'=4,'fsdp_1'=2,'fsdp_2'=4] {'fsdp_1'}, dimensions={0}, use_global_device_ids=true | all-gather | bytes 36864 | tf_op jit(solution)/shard_map/all_gather | solution.py:23
  312.3 12.1 %all-gather.18 = f32[4,2,1536]{2,1,0:T(2,128)S(1)} all-gather(f32[1,2,1536]{2,1,0:T(2,128)S(1)} %maximum_bitcast_fusion.4), channel_id=7, replica_groups=mesh['vocab_0'=2,'vocab_1'=2,'fsdp_0'=4,'fsdp_1'=2,'fsdp_2'=4] {'fsdp_2'}, dimensions={0}, use_global_device_ids=true | all-gather | bytes 61440 | tf_op jit(solution)/shard_map/all_gather | solution.py:23
  324.4 0.1 slice_reduce_fusion.11
  324.6 12.0 %fusion = f32[4096,512]{0,1:T(8,128)} fusion(bf16[1,1536,4096]{2,1,0:T(8,128)(2,1)} %all-gather.29.cloned.1.call-done, f32[1536,512]{0,1:T(8,128)S(1)} %copy-done.2, s32[1536]{0:T(1024)S(1)} %get-tuple-element.22, f32[1536]{0:T(1024)S(1)} %get-tuple-element.36, f32[1536]{0:T(1024)S(1)} %get-tuple-element.37, s32[512]{0:T(512)S(1)} %iota_add_fusion), kind=kOutput, calls=%fused_computation | convolution fusion | flops 6447169536 | bytes 24137728 | tf_op jit(solution)/shard_map/dot_general | solution.py:75
  336.6 19.9 %multiply_reduce_fusion = (f32[4096]{0:T(1024)S(1)}, f32[4096,512]{0,1:T(8,128)}) fusion(bf16[4096,512]{0,1:T(8,128)(2,1)S(1)} %copy-done, f32[4096,512]{0,1:T(8,128)} %copy.11, f32[4096,512]{0,1:T(8,128)} %fusion, bf16[1,1536,4096]{2,1,0:T(8,128)(2,1)} %all-gather.27.cloned.1.call-done, f32[1536,512]{0,1:T(8,128)} %copy-done.3, ...), kind=kOutput, calls=%fused_computation.11 | convolution fusion | flops 6466039808 | bytes 45125632 | tf_op jit(solution)/shard_map/dot_general | solution.py:75
  356.5 62.8 %psum.7 = f32[4096]{0:T(1024)S(1)} all-reduce(f32[4096]{0:T(1024)S(1)} %get-tuple-element.48), channel_id=1, replica_groups=mesh['vocab_0'=2,'vocab_1'=2,'fsdp_0'=4,'fsdp_1'=2,'fsdp_2'=4] {'vocab_0..., use_global_device_ids=true, to_apply=%region_6.7 | all-reduce | flops 4096 | bytes 32768 | tf_op jit(solution)/shard_map/psum | solution.py:80
  419.3 9.0 %copy.13 = f32[4096,512]{1,0:T(8,128)} copy(f32[4096,512]{0,1:T(8,128)} %get-tuple-element.49) | data formatting | bytes 16777216
  428.3 0.6 fusion.25
  (51 shorter events, 0.9 us)
Async XLA Ops:
  7.2 194.7 %all-gather.29.cloned.1.call-start = ((), (), s32[]{:S(2)}) async-start(), calls=%async_computation.1 | async-start | bytes 12976128 | tf_op jit(solution)/shard_map/all_gather | solution.py:65
  11.7 265.0 %all-gather.27.cloned.1.call-start = ((), (), s32[]{:S(2)}) async-start(), calls=%async_computation | async-start | bytes 12976128 | tf_op jit(solution)/shard_map/all_gather | solution.py:65
  18.9 9.0 %copy-start.7 = (u32[128]{0:T(128)S(1)}, u32[128]{0:T(128)}, u32[]{:S(2)}) copy-start(u32[128]{0:T(128)} %constant.55) | copy-start | bytes 1540
  18.9 10.2 %copy-start.6 = (s32[2,48]{1,0:T(2,128)S(1)}, s32[2,48]{1,0:T(2,128)}, u32[]{:S(2)}) copy-start(s32[2,48]{1,0:T(2,128)} %param.8) | copy-start | bytes 1156
  212.7 1.8 copy-start.1
  287.3 49.3 %copy-start.3 = (f32[1536,512]{0,1:T(8,128)}, f32[1536,512]{0,1:T(8,128)S(1)}, u32[]{:S(2)}) copy-start(f32[1536,512]{0,1:T(8,128)S(1)} %get-tuple-element.55) | copy-start | bytes 9437188
  287.3 37.3 %copy-start.2 = (f32[1536,512]{0,1:T(8,128)S(1)}, f32[1536,512]{0,1:T(8,128)}, u32[]{:S(2)}) copy-start(f32[1536,512]{0,1:T(8,128)} %copy-done.1) | copy-start | bytes 9437188
  324.6 12.0 %copy-start = (bf16[4096,512]{0,1:T(8,128)(2,1)S(1)}, bf16[4096,512]{0,1:T(8,128)(2,1)}, u32[]{:S(2)}) copy-start(bf16[4096,512]{0,1:T(8,128)(2,1)} %copy.12) | copy-start | bytes 12582916
  419.3 9.0 %copy-start.4 = (bf16[4096]{0:T(1024)(128)(2,1)S(1)}, bf16[4096]{0:T(1024)(128)(2,1)}, u32[]{:S(2)}) copy-start(bf16[4096]{0:T(1024)(128)(2,1)} %param.7) | copy-start | bytes 24580
  419.3 9.0 %copy-start.5 = (f32[4096]{0:T(1024)S(1)}, f32[4096]{0:T(1024)}, u32[]{:S(2)}) copy-start(f32[4096]{0:T(1024)} %param.11) | copy-start | bytes 49156
Sparse Core Ops, SparseCore 0:
  11.8 133.0 all-gather.28
  147.8 128.7 all-gather.26
where the time goes:
time: 437 us; the launch traced here: 436 us
  blocking collectives  319 us (73%)
  matrix products  53.3 us (12%)
  local copies, waits for them, and re-layouts  28.2 us (6%)
  between operations  14.9 us (3%)
  waiting for transfers between devices  14.5 us (3%)
  other arithmetic  5.6 us (1%)
    unnamed x1, blocking collectives  172 us
    all_gather x10, blocking collectives, gathered_once(): both, at, found = (lax.all_gather(jnp.concatenate(lines), axis), 0, {})  83.8 us
    psum x1, blocking collectives, on_device(): gain_grad = lax.psum(partial_sum, VOCAB_FSDP) / gain_wide  62.8 us
    dot_general x2, matrix products, on_device(): lax.dot_general(rows_all, slope, (((0,), (0,)), ((), ())), preferred_elem...  31.8 us
    unnamed x24, local copies, waits for them, and re-layouts  26.9 us
    dot_general x2, matrix products, on_device(): logits = jnp.dot(rows_all, head_weight, preferred_element_type=jnp.float32)  21.5 us
    all_gather x2, waiting for transfers between devices, on_device(): lax.all_gather(batch_rows, FSDP, axis=0, tiled=True)  13.8 us
  transfers between devices with their start and end apart: 2, of which 1 were waited for; matrix products, arithmetic and copies ran while one was open for 6% of the time, Pallas kernels for 0%

commit v1 on v0

v1 whole, which is shorter than its diff:
```python
import functools

import jax
import jax.numpy as jnp
from jax import lax
from jax.experimental import pallas as pl
from jax.experimental.pallas import tpu as pltpu
from jax.sharding import Mesh
from jax.sharding import PartitionSpec as P

AXES = ("zl", "co", "y", "zh", "x")
SIZES = (2, 2, 4, 2, 4)
VOCAB_FSDP = AXES
FSDP = ("y", "zh", "x")

BETA = 0.99
EPS = 1e-05
LANES = 128
ROWS = 16
SETS = (2, 1)
CALLS = (((0, 0),), ((0, 1), (0, 3), (1, 0)), ((0, 2), (1, 1), (1, 3)), ((1, 2),))
TILE = 256
DBLOCK = 512
PART = 256
FORWARD_LIMIT = 16 * 1024 * 1024
VMEM_LIMIT = 60 * 1024 * 1024


def moved(value, target):
    pairs = []
    for source in range(128):
        rest, at = source, []
        for size in reversed(SIZES):
            at.append(rest % size)
            rest //= size
        to = 0
        for size, coordinate in zip(SIZES, target(*reversed(at))):
            to = to * size + coordinate % size
        pairs.append((source, to))
    return lax.ppermute(value, AXES, pairs)


def z_swap(value):
    return moved(value, lambda zl, co, y, zh, x: (1 - zl, co, y, 1 - zh, x))


def core_swap(value):
    return moved(value, lambda zl, co, y, zh, x: (zl, 1 - co, y, zh, x))


def shift(value, step, phase):
    def target(zl, co, y, zh, x):
        if co == phase:
            return (zl, co, y, zh, x + step)
        return (zl, co, y + step, zh, x)

    return moved(value, target)


PAIRINGS = (
    lambda zl, co, y, zh, x: (zl, 1 - co, y, zh, x),
    lambda zl, co, y, zh, x: (1 - zl, co, y, zh, x),
    lambda zl, co, y, zh, x: (1 - zl, co, y, 1 - zh, x),
    lambda zl, co, y, zh, x: (zl, co, y, zh, x ^ 1),
    lambda zl, co, y, zh, x: (zl, co, y, zh, 3 - x),
    lambda zl, co, y, zh, x: (zl, co, y ^ 1, zh, x),
    lambda zl, co, y, zh, x: (zl, co, 3 - y, zh, x),
)


def log_sum(one, two):
    top = jnp.maximum(one, two)
    return top + jnp.log(jnp.exp(one - top) + jnp.exp(two - top))


def slab_of(two, right, far, left):
    groups, _, _, width = two.shape
    return jnp.stack([two, right, far, left], axis=1).reshape(groups * LANES, width)


def forward_kernel(features, sizes, wt_ref, *refs):
    count = len(sizes)
    x_refs, e_ref, stats_ref = refs[:count], refs[count], refs[count + 1]
    picks = lax.broadcasted_iota(jnp.int32, (ROWS, LANES), 0) == lax.broadcasted_iota(jnp.int32, (ROWS, LANES), 1)
    picks = jnp.where(picks, 1.0, 0.0).astype(jnp.bfloat16)
    across = (((1,), (1,)), ((), ()))
    starts = [sum(sizes[:k]) for k in range(count)]
    for at in range(0, sum(sizes), TILE):
        held = [
            (ref, slice(max(at - start, 0), min(at + TILE - start, size)))
            for ref, start, size in zip(x_refs, starts, sizes)
            if start < at + TILE and at < start + size
        ]

        def rows_of(cols):
            parts = [ref[part, cols] for ref, part in held]
            return parts[0] if len(parts) == 1 else jnp.concatenate(parts, axis=0)

        rows = slice(at, at + TILE)
        logits = lax.dot_general(
            wt_ref[...], rows_of(slice(0, features)), across, preferred_element_type=jnp.float32
        )
        top = jnp.max(logits, axis=0, keepdims=True)
        e = jnp.exp(logits - top)
        total = jnp.sum(e, axis=0, keepdims=True)
        e_ref[:, rows] = e
        codes = lax.dot_general(
            picks, rows_of(slice(features, features + LANES)), across, preferred_element_type=jnp.float32
        )
        label = codes[0:1] * 256.0 + codes[1:2]
        for part in range(TILE // LANES):
            row = at // LANES + part
            cols = slice(part * LANES, (part + 1) * LANES)
            stats_ref[0, row : row + 1, :] = top[:, cols]
            stats_ref[1, row : row + 1, :] = total[:, cols]
            stats_ref[2, row : row + 1, :] = label[:, cols]


def forward(wt, buffers, features):
    columns = wt.shape[0]
    sizes = [b.shape[0] for b in buffers]
    tokens = sum(sizes)
    width = buffers[0].shape[1]
    vmem = pl.BlockSpec(memory_space=pltpu.VMEM)
    return pl.pallas_call(
        functools.partial(forward_kernel, features, sizes),
        out_shape=(
            jax.ShapeDtypeStruct((columns, tokens), jnp.float32),
            jax.ShapeDtypeStruct((3, tokens // LANES, LANES), jnp.float32),
        ),
        in_specs=[vmem] * (1 + len(buffers)),
        out_specs=(vmem, vmem),
        compiler_params=pltpu.CompilerParams(vmem_limit_bytes=FORWARD_LIMIT),
        cost_estimate=pl.CostEstimate(
            flops=2 * columns * tokens * features,
            bytes_accessed=2 * tokens * width + 2 * columns * features + 4 * columns * tokens,
            transcendentals=columns * tokens,
        ),
        name="forward",
    )(wt, *buffers)


def aligned(block, lead, zh):
    lane = lax.broadcasted_iota(jnp.int32, block.shape, block.ndim - 1)
    back = pltpu.roll(block, LANES - ROWS, block.ndim - 1)
    ahead = pltpu.roll(block, ROWS, block.ndim - 1)
    swapped = jnp.where((lane // ROWS) % 2 == 0, back, ahead)
    block = jnp.where(zh == 1, swapped, block)
    turned = block
    for k in range(1, 4):
        turned = jnp.where(lead == k, pltpu.roll(block, k * 2 * ROWS, block.ndim - 1), turned)
    return turned


def place_of(place_ref, which):
    core, y, zh, x = (place_ref[k] for k in range(4))
    part = core if which == 0 else 1 - core
    return part, jnp.where(part == 0, y, x), jnp.where(part == 0, x, y), zh


def layout():
    found = {}
    for call, slabs in enumerate(CALLS):
        row = 0
        for which in range(2):
            for part, slab in slabs:
                found[part, which, slab] = (call, row)
                row += SETS[part]
    return found


def first_row(part):
    return sum(8 * groups for groups in SETS[:part])


def canon_kernel(place_ref, *refs):
    stats_refs, out_ref, turned = refs[: len(CALLS)], refs[-2], refs[-1]
    at = layout()
    for part, groups in enumerate(SETS):
        for which in range(2):
            batch, slab0, lane0, zh = place_of(place_ref, which)
            for slab in range(4):
                call, row = at[part, which, slab]
                ref = stats_refs[call]
                sums = ref[0, row : row + groups, :] + jnp.log(ref[1, row : row + groups, :])
                turned[slab * groups : (slab + 1) * groups, :] = sums
            turned[: 4 * groups, :] = aligned(turned[: 4 * groups, :], lane0, zh)
            for slab in range(4):
                to = first_row(part) + (batch * 4 + lax.rem(slab0 + slab, 4)) * groups
                for g in range(groups):
                    row = slab * groups + g
                    out_ref[pl.ds(to + g, 1), :] = turned[row : row + 1, :]


def canonical(place, stats):
    return pl.pallas_call(
        canon_kernel,
        out_shape=jax.ShapeDtypeStruct((first_row(len(SETS)), LANES), jnp.float32),
        in_specs=[pl.BlockSpec(memory_space=pltpu.SMEM)] + [pl.BlockSpec(memory_space=pltpu.VMEM)] * len(stats),
        out_specs=pl.BlockSpec(memory_space=pltpu.VMEM),
        scratch_shapes=[pltpu.VMEM((4 * max(SETS), LANES), jnp.float32)],
        name="canonical",
    )(place, *stats)


def backward_kernel(sizes, widths, count, place_ref, base_ref, *refs):
    calls, buffers = len(CALLS), len(sizes)
    stats_refs, joined_ref, wt_ref, ema_ref = refs[:calls], refs[calls], refs[calls + 1], refs[calls + 2]
    e_refs = refs[calls + 3 : 2 * calls + 3]
    x_refs = refs[2 * calls + 3 : 2 * calls + 3 + buffers]
    new_ref, gain_ref, xs, es, slope, rel, sems, e_sems = refs[2 * calls + 3 + buffers :]
    step, steps = pl.program_id(0), pl.num_programs(0)

    def copies(block, slot):
        at, made = 0, []
        cols = pl.ds(pl.multiple_of(block * DBLOCK, DBLOCK), DBLOCK)
        for k, size in enumerate(sizes):
            made.append(pltpu.make_async_copy(x_refs[k].at[:, cols], xs.at[slot, pl.ds(at, size)], sems.at[slot, k]))
            at += size
        return made

    @pl.when(step == 0)
    def _():
        starts = [sum(widths[:call]) for call in range(calls)]
        e_copies = [
            pltpu.make_async_copy(e_refs[call], es.at[:, pl.ds(starts[call], widths[call])], e_sems.at[call])
            for call in range(calls)
        ]
        for copy in e_copies + copies(0, 0):
            copy.start()
        at = layout()
        columns = es.shape[0]
        ids = lax.broadcasted_iota(jnp.int32, (columns, LANES), 0) + base_ref[0]
        for part, groups in enumerate(SETS):
            for which in range(2):
                batch, slab0, lane0, zh = place_of(place_ref, which)
                for slab in range(4):
                    row = first_row(part) + (batch * 4 + lax.rem(slab0 + slab, 4)) * groups
                    call, to = at[part, which, slab]
                    to += starts[call] // LANES
                    for g in range(groups):
                        rel[to + g : to + g + 1, :] = aligned(joined_ref[pl.ds(row + g, 1), :], lax.rem(4 - lane0, 4), zh)
        for call in range(calls):
            e_copies[call].wait()
            for row in range(widths[call] // LANES):
                k = starts[call] // LANES + row
                cols = slice(k * LANES, (k + 1) * LANES)
                scale = jnp.exp(stats_refs[call][0, row : row + 1, :] - rel[k : k + 1, :])
                hits = ids == stats_refs[call][2, row : row + 1, :].astype(jnp.int32)
                slope[:, cols] = (es[:, cols] * scale - jnp.where(hits, 1.0, 0.0)).astype(jnp.bfloat16)

    @pl.when(step + 1 < steps)
    def _():
        for copy in copies(step + 1, lax.rem(step + 1, 2)):
            copy.start()

    slot = lax.rem(step, 2)
    for copy in copies(step, slot):
        copy.wait()
    for k in range(DBLOCK // PART):
        cols = slice(k * PART, (k + 1) * PART)
        gradient = jnp.dot(slope[...], xs[slot, :, cols], preferred_element_type=jnp.float32)
        gain_ref[:, cols] = jnp.sum(wt_ref[:, cols].astype(jnp.float32) * gradient, axis=0, keepdims=True)
        turned = gradient.T
        new_ref[cols, :] = BETA * ema_ref[cols, :] + (1.0 - BETA) * turned * turned / count


def backward(place, base, stats, joined, es, wt, ema, buffers, count):
    features, columns = ema.shape
    sizes = [b.shape[0] for b in buffers]
    widths = [e.shape[1] for e in es]
    tokens = sum(sizes)
    whole = pl.BlockSpec(memory_space=pltpu.VMEM)
    return pl.pallas_call(
        functools.partial(backward_kernel, sizes, widths, count),
        grid=(features // DBLOCK,),
        out_shape=(
            jax.ShapeDtypeStruct((features, columns), jnp.float32),
            jax.ShapeDtypeStruct((1, features), jnp.float32),
        ),
        in_specs=[
            pl.BlockSpec(memory_space=pltpu.SMEM),
            pl.BlockSpec(memory_space=pltpu.SMEM),
            *[whole] * (len(stats) + 1),
            pl.BlockSpec((columns, DBLOCK), lambda j: (0, j)),
            pl.BlockSpec((DBLOCK, columns), lambda j: (j, 0)),
        ]
        + [pl.BlockSpec(memory_space=pl.ANY)] * (len(es) + len(buffers)),
        out_specs=(
            pl.BlockSpec((DBLOCK, columns), lambda j: (j, 0)),
            pl.BlockSpec((1, DBLOCK), lambda j: (0, j)),
        ),
        scratch_shapes=[
            pltpu.VMEM((2, tokens, DBLOCK), jnp.bfloat16),
            pltpu.VMEM((columns, tokens), jnp.float32),
            pltpu.VMEM((columns, tokens), jnp.bfloat16),
            pltpu.VMEM((tokens // LANES, LANES), jnp.float32),
            pltpu.SemaphoreType.DMA((2, len(buffers))),
            pltpu.SemaphoreType.DMA((len(es),)),
        ],
        compiler_params=pltpu.CompilerParams(
            vmem_limit_bytes=VMEM_LIMIT, dimension_semantics=("arbitrary",)
        ),
        cost_estimate=pl.CostEstimate(
            flops=2 * columns * tokens * features,
            bytes_accessed=2 * tokens * features + 10 * columns * features + 4 * columns * tokens,
            transcendentals=0,
        ),
        name="backward",
    )(place, base, *stats, joined, wt, ema, *es, *buffers)


def on_device(hidden, norm_gain, labels, head_weight, head_ema, gain_ema):
    batches, own_rows, features = hidden.shape
    columns = head_weight.shape[1]
    core = lax.axis_index("co")
    place = jnp.stack([core, lax.axis_index("y"), lax.axis_index("zh"), lax.axis_index("x")]).astype(jnp.int32)
    base = (lax.axis_index(VOCAB_FSDP) * columns).astype(jnp.int32).reshape(1)
    gain_wide = norm_gain.astype(jnp.float32)
    wide = lax.dynamic_index_in_dim(hidden, core, 0, keepdims=False).astype(jnp.float32)
    factor = lax.rsqrt(jnp.mean(wide * wide, axis=-1, keepdims=True) + EPS)
    scaled = (wide * factor * gain_wide).astype(jnp.bfloat16)
    own_labels = lax.dynamic_index_in_dim(labels, core, 0, keepdims=False)[:, None]
    lane = lax.broadcasted_iota(jnp.int32, (own_rows, LANES), 1)
    codes = jnp.where(lane == 0, own_labels // 256, jnp.where(lane == 1, own_labels % 256, 0)).astype(jnp.bfloat16)
    own = jnp.concatenate([scaled, codes], axis=1).reshape(own_rows // ROWS, ROWS, features + LANES)
    count = batches * own_rows * 32
    wt = head_weight.T

    tie = lax.optimization_barrier
    own0, own1 = own[: SETS[0]], own[SETS[0] :]
    z0, z1 = z_swap(own0), z_swap(own1)
    two0 = jnp.stack([own0, z0], axis=1)
    left0, right0 = shift(two0, 1, 0), shift(two0, -1, 0)
    left0, right0, z1, wt = tie((left0, right0, z1, wt))
    two1 = jnp.stack([own1, z1], axis=1)
    far0 = [shift(left0[:, :1], 1, 0), shift(right0[:, 1:], -1, 0)]
    left1, right1 = shift(two1, 1, 0), shift(two1, -1, 0)
    first0 = slab_of(two0, right0, jnp.concatenate(far0, axis=1), left0)
    a_left0, a_right0 = shift(first0, 1, 1), shift(first0, -1, 1)
    far1 = [shift(left1[:, :1], 1, 0), shift(right1[:, 1:], -1, 0)]
    theirs0 = core_swap(first0)
    out0 = forward(wt, [first0, theirs0], features)
    first1 = slab_of(two1, right1, jnp.concatenate(far1, axis=1), left1)
    a_left0, a_right0, first1, out0 = tie((a_left0, a_right0, first1, out0))
    half0, half1 = SETS[0] * LANES // 2, SETS[1] * LANES // 2
    a_far0 = [shift(a_left0[:half0], 1, 1), shift(a_right0[half0:], -1, 1)]
    mine = [[first0], [a_right0, a_left0, first1]]
    theirs = [[theirs0], [core_swap(b) for b in mine[1]]]
    ahead1, theirs[1] = tie((first1, theirs[1]))
    a_left1, a_right1 = shift(ahead1, 1, 1), shift(ahead1, -1, 1)
    out1 = forward(wt, mine[1] + theirs[1], features)
    a_left1, a_right1, out1 = tie((a_left1, a_right1, out1))
    a_far1 = [shift(a_left1[:half1], 1, 1), shift(a_right1[half1:], -1, 1)]
    mine += [a_far0 + [a_right1, a_left1]]
    theirs += [[core_swap(b) for b in mine[2]]]
    out2 = forward(wt, mine[2] + theirs[2], features)
    a_far1[0], a_far1[1], out2 = tie((a_far1[0], a_far1[1], out2))
    theirs += [[core_swap(b) for b in a_far1]]
    mine += [a_far1]
    out3 = forward(wt, a_far1 + theirs[3], features)
    es, stats = zip(out0, out1, out2, out3)
    joined = canonical(place, stats)
    for pairing in PAIRINGS:
        joined = log_sum(joined, moved(joined, pairing))
    buffers = [b for pair in zip(mine, theirs) for side in pair for b in side]
    head_new, partial_sum = backward(place, base, stats, joined, es, wt, head_ema, buffers, count)
    for pairing in PAIRINGS:
        partial_sum = partial_sum + moved(partial_sum, pairing)
    gain_grad = partial_sum[0] / gain_wide
    gain_new = BETA * gain_ema + (1.0 - BETA) * gain_grad * gain_grad / count
    return (head_new, gain_new)


def solution(mesh):
    finer = Mesh(mesh.devices.reshape(SIZES), AXES)
    return jax.shard_map(
        on_device,
        mesh=finer,
        in_specs=(
            P(None, FSDP, None),
            P(),
            P(None, FSDP),
            P(None, VOCAB_FSDP),
            P(None, VOCAB_FSDP),
            P(),
        ),
        out_specs=(P(None, VOCAB_FSDP), P()),
        check_vma=False,
    )
```

time: 437 us -> 210 us (0.48)
  blocking collectives: 319 us -> 0 us
  waiting for transfers between devices: 14.5 us -> 106 us
  matrix products: 53.3 us -> 0 us
  Pallas kernels: 0 us -> 42.9 us
  starting transfers between devices: 0.08 us -> 35.9 us
  between operations: 14.9 us -> 1.22 us
  local copies, waits for them, and re-layouts: 28.2 us -> 15.3 us
    unnamed x1 -> x0, blocking collectives: 172 us -> none
    ppermute x0 -> x42, waiting for transfers between devices: none -> 106 us  [moved(): return lax.ppermute(value, AXES, pairs)]
    all_gather x10 -> x0, blocking collectives: 83.8 us -> none  [gathered_once(): both, at, found = (lax.all_gather(jnp.concatenate(lines), axis), 0, {})]
    psum x1 -> x0, blocking collectives: 62.8 us -> none  [on_device(): gain_grad = lax.psum(partial_sum, VOCAB_FSDP) / gain_wide]
    dot_general x4 -> x0, matrix products: 53.3 us -> none  [the longest x2 31.8 us: on_device(): lax.dot_general(rows_all, slope, (((0,), (0,)), ((), ())), preferred_elem...]
    pallas_call x0 -> x6, Pallas kernels: none -> 42.9 us  [the longest x1 25.7 us: backward(): pl.pallas_call(functools.partial(backward_kernel, sizes, widths, count),...]
    ppermute x0 -> x42, starting transfers between devices: none -> 35.9 us  [moved(): return lax.ppermute(value, AXES, pairs)]
    all_gather x2 -> x0, waiting for transfers between devices: 13.8 us -> none  [on_device(): lax.all_gather(batch_rows, FSDP, axis=0, tiled=True)]
  transfers between devices with their start and end apart: 2 -> 42, of which waited for: 1 -> 29; matrix products, arithmetic and copies ran while one was open for 6% -> 4% of each run, Pallas kernels for 0% -> 7%
where the time goes in v1:
time: 210 us
  waiting for transfers between devices  106 us (50%)
  Pallas kernels  42.9 us (20%)
  starting transfers between devices  35.9 us (17%)
  local copies, waits for them, and re-layouts  15.3 us (7%)
  other arithmetic  8.1 us (4%)
    ppermute x42, waiting for transfers between devices, moved(): return lax.ppermute(value, AXES, pairs)  106 us
    ppermute x42, starting transfers between devices, moved(): return lax.ppermute(value, AXES, pairs)  35.9 us
    pallas_call x1, Pallas kernels, backward(): pl.pallas_call(functools.partial(backward_kernel, sizes, widths, count),...  25.7 us
    pallas_call x4, Pallas kernels, forward(): pl.pallas_call(functools.partial(forward_kernel, features, sizes), out_sh...  15.2 us
    unnamed x65, local copies, waits for them, and re-layouts  15 us
  transfers between devices with their start and end apart: 42, of which 29 were waited for; matrix products, arithmetic and copies ran while one was open for 4% of the time, Pallas kernels for 7%

profile of v1, /device:TPU:6, one launch (start us, length us, event | category | flops | bytes accessed | tf_op | source)
XLA Modules:
  0.0 209.8 jit_solution(15684909479865859568)
XLA Ops:
  4.5 4.1 %collective-permute-start = (bf16[2,16,4224]{2,1,0:T(8,128)(2,1)S(1)}, bf16[2,16,4224]{2,1,0:T(8,128)(2,1)S(1)}, u32[]{:S(2)}, u32[]{:S(2)}) collective-permute-start(bf16[2,16,4224]{2,1,0:T(8,128)(2,1)S(1)} %bitcast.70), channel_id=1, source_target_pairs={{0,68},{1,69},{2,70},{3,71},{4,64},{5,65},{6,66},{7,67},{8,76},{9,... | collective-permute-start | bytes 811016 | tf_op jit(solution)/shard_map/ppermute | solution.py:40
  8.6 6.5 %collective-permute-done = bf16[2,16,4224]{2,1,0:T(8,128)(2,1)S(1)} collective-permute-done((bf16[2,16,4224]{2,1,0:T(8,128)(2,1)S(1)}, bf16[2,16,4224]{2,1,0:T(8,128)(2,1)S(1)}, u32[]{:S(2)}, u32[]{:S(2)}) %collective-permute-start) | collective-permute-done | bytes 270368 | tf_op jit(solution)/shard_map/ppermute | solution.py:40
  20.3 6.4 %copy.9 = bf16[4096,512]{0,1:T(8,128)(2,1)} copy(bf16[4096,512]{1,0:T(8,128)(2,1)} %param.9) | data formatting | bytes 8388608 | tf_op args[3]
  28.9 4.4 %collective-permute-done.4 = bf16[2,1,16,4224]{3,2,1,0:T(8,128)(2,1)S(1)} collective-permute-done((bf16[2,1,16,4224]{3,2,1,0:T(8,128)(2,1)S(1)}, bf16[2,1,16,4224]{3,2,1,0:T(8,128)(2,1)S(1)}, u32[]{:S(2)}, u32[]{:S(2)}) %collective-permute-start.4) | collective-permute-done | bytes 270368 | tf_op jit(solution)/shard_map/ppermute | solution.py:40
  36.8 3.1 %collective-permute-start.7 = (bf16[256,4224]{1,0:T(8,128)(2,1)S(1)}, bf16[256,4224]{1,0:T(8,128)(2,1)S(1)}, u32[]{:S(2)}, u32[]{:S(2)}) collective-permute-start(bf16[256,4224]{1,0:T(8,128)(2,1)S(1)} %bitcast.59), channel_id=1, source_target_pairs={{0,24},{1,25},{2,26},{3,27},{4,28},{5,29},{6,30},{7,31},{8,0},{9,1... | collective-permute-start | bytes 6488072 | tf_op jit(solution)/shard_map/ppermute | solution.py:40
  40.0 3.2 %collective-permute-start.9 = (bf16[1,2,16,4224]{3,2,1,0:T(8,128)(2,1)S(1)}, bf16[1,2,16,4224]{3,2,1,0:T(8,128)(2,1)S(1)}, u32[]{:S(2)}, u32[]{:S(2)}) collective-permute-start(bf16[1,2,16,4224]{3,2,1,0:T(8,128)(2,1)S(1)} %get-tuple-element.71), channel_id=1, source_target_pairs={{0,1},{1,2},{2,3},{3,0},{4,5},{5,6},{6,7},{7,4},{8,9},{9,10},{10,1... | collective-permute-start | bytes 811016 | tf_op jit(solution)/shard_map/ppermute | solution.py:40
  43.2 7.4 %collective-permute-done.8 = bf16[1,2,16,4224]{3,2,1,0:T(8,128)(2,1)S(1)} collective-permute-done((bf16[1,2,16,4224]{3,2,1,0:T(8,128)(2,1)S(1)}, bf16[1,2,16,4224]{3,2,1,0:T(8,128)(2,1)S(1)}, u32[]{:S(2)}, u32[]{:S(2)}) %collective-permute-start.8) | collective-permute-done | bytes 270368 | tf_op jit(solution)/shard_map/ppermute | solution.py:40
  50.7 3.3 %collective-permute-start.10 = (bf16[1,1,16,4224]{3,2,1,0:T(8,128)(2,1)S(1)}, bf16[1,1,16,4224]{3,2,1,0:T(8,128)(2,1)S(1)}, u32[]{:S(2)}, u32[]{:S(2)}) collective-permute-start(bf16[1,1,16,4224]{3,2,1,0:T(8,128)(2,1)S(1)} %slice.50), channel_id=1, source_target_pairs={{0,1},{1,2},{2,3},{3,0},{4,5},{5,6},{6,7},{7,4},{8,9},{9,10},{10,1... | collective-permute-start | bytes 405512 | tf_op jit(solution)/shard_map/ppermute | solution.py:40
  54.0 4.4 %collective-permute-done.11 = bf16[1,1,16,4224]{3,2,1,0:T(8,128)(2,1)S(1)} collective-permute-done((bf16[1,1,16,4224]{3,2,1,0:T(8,128)(2,1)S(1)}, bf16[1,1,16,4224]{3,2,1,0:T(8,128)(2,1)S(1)}, u32[]{:S(2)}, u32[]{:S(2)}) %collective-permute-start.11) | collective-permute-done | bytes 135200 | tf_op jit(solution)/shard_map/ppermute | solution.py:40
  62.8 5.6 %collective-permute-done.7.refs_0_.refs_13_ = bf16[256,4224]{1,0:T(8,128)(2,1)S(1)} collective-permute-done((bf16[256,4224]{1,0:T(8,128)(2,1)S(1)}, bf16[256,4224]{1,0:T(8,128)(2,1)S(1)}, u32[]{:S(2)}, u32[]{:S(2)}) %collective-permute-start.7) | collective-permute-done | bytes 2162720 | tf_op jit(solution)/shard_map/ppermute | solution.py:40
  68.5 3.7 %collective-permute-done.6.refs_1_.refs_14_ = bf16[256,4224]{1,0:T(8,128)(2,1)S(1)} collective-permute-done((bf16[256,4224]{1,0:T(8,128)(2,1)S(1)}, bf16[256,4224]{1,0:T(8,128)(2,1)S(1)}, u32[]{:S(2)}, u32[]{:S(2)}) %collective-permute-start.6) | collective-permute-done | bytes 2162720 | tf_op jit(solution)/shard_map/ppermute | solution.py:40
  72.9 3.3 %collective-permute-start.21 = (bf16[128,4224]{1,0:T(8,128)(2,1)S(1)}, bf16[128,4224]{1,0:T(8,128)(2,1)S(1)}, u32[]{:S(2)}, u32[]{:S(2)}) collective-permute-start(bf16[128,4224]{1,0:T(8,128)(2,1)S(1)} %slice.47), channel_id=1, source_target_pairs={{0,24},{1,25},{2,26},{3,27},{4,28},{5,29},{6,30},{7,31},{8,0},{9,1... | collective-permute-start | bytes 3244040 | tf_op jit(solution)/shard_map/ppermute | solution.py:40
  76.2 4.8 %collective-permute-done.15.refs_5_.refs_18_ = bf16[128,4224]{1,0:T(8,128)(2,1)S(1)} collective-permute-done((bf16[128,4224]{1,0:T(8,128)(2,1)S(1)}, bf16[128,4224]{1,0:T(8,128)(2,1)S(1)}, u32[]{:S(2)}, u32[]{:S(2)}) %collective-permute-start.15) | collective-permute-done | bytes 1081376 | tf_op jit(solution)/shard_map/ppermute | solution.py:40
  83.2 6.0 %collective-permute-done.20.refs_0_.refs_19_ = bf16[128,4224]{1,0:T(8,128)(2,1)S(1)} collective-permute-done((bf16[128,4224]{1,0:T(8,128)(2,1)S(1)}, bf16[128,4224]{1,0:T(8,128)(2,1)S(1)}, u32[]{:S(2)}, u32[]{:S(2)}) %collective-permute-start.20) | collective-permute-done | bytes 1081376 | tf_op jit(solution)/shard_map/ppermute | solution.py:40
  89.7 6.2 %forward.5 = (f32[512,1280]{1,0:T(8,128)S(1)}, f32[3,10,128]{2,1,0:T(8,128)S(1)}) custom-call(bf16[512,4096]{1,0:T(8,128)(2,1)S(1)} %bitcast.55, bf16[256,4224]{1,0:T(8,128)(2,1)S(1)} %collective-permute-done.7.refs_0_.refs_13_, bf16[256,4224]{1,0:T(8,128)(2,1)S(1)} %collective-permute-done.6.refs_1_.refs_14_, bf16[128,4224]{1,0:T(8,128)(2,1)S(1)} %bitcast.66, ...), custom_call_target="tpu_custom_call" | custom-call | flops 5368709120 | bytes 17629184 | tf_op jit(solution)/shard_map/forward/pallas_call | solution.py:125
  97.4 3.1 %collective-permute-done.17.refs_2_.refs_21_ = bf16[128,4224]{1,0:T(8,128)(2,1)S(1)} collective-permute-done((bf16[128,4224]{1,0:T(8,128)(2,1)S(1)}, bf16[128,4224]{1,0:T(8,128)(2,1)S(1)}, u32[]{:S(2)}, u32[]{:S(2)}) %collective-permute-start.17) | collective-permute-done | bytes 1081376 | tf_op jit(solution)/shard_map/ppermute | solution.py:40
  101.4 3.5 %collective-permute-start.19 = (bf16[64,4224]{1,0:T(8,128)(2,1)S(1)}, bf16[64,4224]{1,0:T(8,128)(2,1)S(1)}, u32[]{:S(2)}, u32[]{:S(2)}) collective-permute-start(bf16[64,4224]{1,0:T(8,128)(2,1)S(1)} %slice.45), channel_id=1, source_target_pairs={{0,24},{1,25},{2,26},{3,27},{4,28},{5,29},{6,30},{7,31},{8,0},{9,1... | collective-permute-start | bytes 1622024 | tf_op jit(solution)/shard_map/ppermute | solution.py:40
  105.0 5.0 %forward.6 = (f32[512,1024]{1,0:T(8,128)S(1)}, f32[3,8,128]{2,1,0:T(8,128)S(1)}) custom-call(bf16[512,4096]{1,0:T(8,128)(2,1)S(1)} %bitcast.56, bf16[128,4224]{1,0:T(8,128)(2,1)S(1)} %collective-permute-done.20.refs_0_.refs_19_, bf16[128,4224]{1,0:T(8,128)(2,1)S(1)} %collective-permute-done.21.refs_1_.refs_20_, ...), custom_call_target="tpu_custom_call" | custom-call | flops 4294967296 | bytes 14942208 | tf_op jit(solution)/shard_map/forward/pallas_call | solution.py:125
  112.0 3.5 %collective-permute-done.18.refs_0_.refs_27_ = bf16[64,4224]{1,0:T(8,128)(2,1)S(1)} collective-permute-done((bf16[64,4224]{1,0:T(8,128)(2,1)S(1)}, bf16[64,4224]{1,0:T(8,128)(2,1)S(1)}, u32[]{:S(2)}, u32[]{:S(2)}) %collective-permute-start.18) | collective-permute-done | bytes 540704 | tf_op jit(solution)/shard_map/ppermute | solution.py:40
  127.4 3.7 %collective-permute-done.29 = f32[24,128]{1,0:T(8,128)S(1)} collective-permute-done((f32[24,128]{1,0:T(8,128)S(1)}, f32[24,128]{1,0:T(8,128)S(1)}, u32[]{:S(2)}, u32[]{:S(2)}) %collective-permute-start.29) | collective-permute-done | bytes 12320 | tf_op jit(solution)/shard_map/ppermute | solution.py:40
  132.3 3.9 %collective-permute-done.30 = f32[24,128]{1,0:T(8,128)S(1)} collective-permute-done((f32[24,128]{1,0:T(8,128)S(1)}, f32[24,128]{1,0:T(8,128)S(1)}, u32[]{:S(2)}, u32[]{:S(2)}) %collective-permute-start.30) | collective-permute-done | bytes 12320 | tf_op jit(solution)/shard_map/ppermute | solution.py:40
  136.5 3.7 %collective-permute-done.31 = f32[24,128]{1,0:T(8,128)S(1)} collective-permute-done((f32[24,128]{1,0:T(8,128)S(1)}, f32[24,128]{1,0:T(8,128)S(1)}, u32[]{:S(2)}, u32[]{:S(2)}) %collective-permute-start.31) | collective-permute-done | bytes 12320 | tf_op jit(solution)/shard_map/ppermute | solution.py:40
  140.3 4.9 %collective-permute-done.32 = f32[24,128]{1,0:T(8,128)S(1)} collective-permute-done((f32[24,128]{1,0:T(8,128)S(1)}, f32[24,128]{1,0:T(8,128)S(1)}, u32[]{:S(2)}, u32[]{:S(2)}) %collective-permute-start.32) | collective-permute-done | bytes 12320 | tf_op jit(solution)/shard_map/ppermute | solution.py:40
  145.3 3.7 %collective-permute-done.33 = f32[24,128]{1,0:T(8,128)S(1)} collective-permute-done((f32[24,128]{1,0:T(8,128)S(1)}, f32[24,128]{1,0:T(8,128)S(1)}, u32[]{:S(2)}, u32[]{:S(2)}) %collective-permute-start.33) | collective-permute-done | bytes 12320 | tf_op jit(solution)/shard_map/ppermute | solution.py:40
  149.1 4.8 %collective-permute-done.34 = f32[24,128]{1,0:T(8,128)S(1)} collective-permute-done((f32[24,128]{1,0:T(8,128)S(1)}, f32[24,128]{1,0:T(8,128)S(1)}, u32[]{:S(2)}, u32[]{:S(2)}) %collective-permute-start.34) | collective-permute-done | bytes 12320 | tf_op jit(solution)/shard_map/ppermute | solution.py:40
  154.6 25.7 %backward.1 = (f32[4096,512]{1,0:T(8,128)}, f32[1,4096]{1,0:T(1,128)}) custom-call(s32[4]{0:T(128)} %pad_add_fusion.place_ref, s32[1]{0:T(128)} %bitcast.4.base_ref, f32[3,4,128]{2,1,0:T(4,128)} %copy-done.15, f32[3,10,128]{2,1,0:T(8,128)} %copy-done.13, f32[3,8,128]{2,1,0:T(8,128)} %copy-done.14, f32[3,2,128]{2,1,0:T(2,128)} %copy-done.16, ...), custom_call_target="tpu_custom_call" | custom-call | flops 12884901888 | bytes 52428800 | tf_op jit(solution)/shard_map/backward/pallas_call | solution.py:274
  182.6 3.7 %collective-permute-done.36 = f32[1,4096]{1,0:T(1,128)S(1)} collective-permute-done((f32[1,4096]{1,0:T(1,128)S(1)}, f32[1,4096]{1,0:T(1,128)S(1)}, u32[]{:S(2)}, u32[]{:S(2)}) %collective-permute-start.36) | collective-permute-done | bytes 16416 | tf_op jit(solution)/shard_map/ppermute | solution.py:40
  187.5 3.9 %collective-permute-done.37 = f32[1,4096]{1,0:T(1,128)S(1)} collective-permute-done((f32[1,4096]{1,0:T(1,128)S(1)}, f32[1,4096]{1,0:T(1,128)S(1)}, u32[]{:S(2)}, u32[]{:S(2)}) %collective-permute-start.37) | collective-permute-done | bytes 16416 | tf_op jit(solution)/shard_map/ppermute | solution.py:40
  191.5 3.7 %collective-permute-done.38 = f32[1,4096]{1,0:T(1,128)S(1)} collective-permute-done((f32[1,4096]{1,0:T(1,128)S(1)}, f32[1,4096]{1,0:T(1,128)S(1)}, u32[]{:S(2)}, u32[]{:S(2)}) %collective-permute-start.38) | collective-permute-done | bytes 16416 | tf_op jit(solution)/shard_map/ppermute | solution.py:40
  195.4 4.9 %collective-permute-done.39 = f32[1,4096]{1,0:T(1,128)S(1)} collective-permute-done((f32[1,4096]{1,0:T(1,128)S(1)}, f32[1,4096]{1,0:T(1,128)S(1)}, u32[]{:S(2)}, u32[]{:S(2)}) %collective-permute-start.39) | collective-permute-done | bytes 16416 | tf_op jit(solution)/shard_map/ppermute | solution.py:40
  200.4 3.7 %collective-permute-done.40 = f32[1,4096]{1,0:T(1,128)S(1)} collective-permute-done((f32[1,4096]{1,0:T(1,128)S(1)}, f32[1,4096]{1,0:T(1,128)S(1)}, u32[]{:S(2)}, u32[]{:S(2)}) %collective-permute-start.40) | collective-permute-done | bytes 16416 | tf_op jit(solution)/shard_map/ppermute | solution.py:40
  204.3 4.8 %collective-permute-done.41 = f32[1,4096]{1,0:T(1,128)S(1)} collective-permute-done((f32[1,4096]{1,0:T(1,128)S(1)}, f32[1,4096]{1,0:T(1,128)S(1)}, u32[]{:S(2)}, u32[]{:S(2)}) %collective-permute-start.41) | collective-permute-done | bytes 16416 | tf_op jit(solution)/shard_map/ppermute | solution.py:40
  (163 shorter events, 45.9 us)
Async XLA Ops:
  4.5 10.6 %collective-permute-start = (bf16[2,16,4224]{2,1,0:T(8,128)(2,1)S(1)}, bf16[2,16,4224]{2,1,0:T(8,128)(2,1)S(1)}, u32[]{:S(2)}, u32[]{:S(2)}) collective-permute-start(bf16[2,16,4224]{2,1,0:T(8,128)(2,1)S(1)} %bitcast.70), channel_id=1, source_target_pairs={{0,68},{1,69},{2,70},{3,71},{4,64},{5,65},{6,66},{7,67},{8,76},{9,... | collective-permute-start | bytes 811016 | tf_op jit(solution)/shard_map/ppermute | solution.py:40
  15.2 11.6 %collective-permute-start.1 = (bf16[2,2,16,4224]{3,2,1,0:T(8,128)(2,1)S(1)}, bf16[2,2,16,4224]{3,2,1,0:T(8,128)(2,1)S(1)}, u32[]{:S(2)}, u32[]{:S(2)}) collective-permute-start(bf16[2,2,16,4224]{3,2,1,0:T(8,128)(2,1)S(1)} %get-tuple-element.67), channel_id=1, source_target_pairs={{0,1},{1,2},{2,3},{3,0},{4,5},{5,6},{6,7},{7,4},{8,9},{9,10},{10,1... | collective-permute-start | bytes 1622024 | tf_op jit(solution)/shard_map/ppermute | solution.py:40
  15.7 11.0 %collective-permute-start.2 = (bf16[2,2,16,4224]{3,2,1,0:T(8,128)(2,1)S(1)}, bf16[2,2,16,4224]{3,2,1,0:T(8,128)(2,1)S(1)}, u32[]{:S(2)}, u32[]{:S(2)}) collective-permute-start(bf16[2,2,16,4224]{3,2,1,0:T(8,128)(2,1)S(1)} %get-tuple-element.67), channel_id=1, source_target_pairs={{0,3},{1,0},{2,1},{3,2},{4,7},{5,4},{6,5},{7,6},{8,11},{9,8},{10,9... | collective-permute-start | bytes 1622024 | tf_op jit(solution)/shard_map/ppermute | solution.py:40
  17.3 9.5 %collective-permute-start.3 = (bf16[1,16,4224]{2,1,0:T(8,128)(2,1)S(1)}, bf16[1,16,4224]{2,1,0:T(8,128)(2,1)S(1)}, u32[]{:S(2)}, u32[]{:S(2)}) collective-permute-start(bf16[1,16,4224]{2,1,0:T(8,128)(2,1)S(1)} %get-tuple-element.69), channel_id=1, source_target_pairs={{0,68},{1,69},{2,70},{3,71},{4,64},{5,65},{6,66},{7,67},{8,76},{9,... | collective-permute-start | bytes 405512 | tf_op jit(solution)/shard_map/ppermute | solution.py:40
  26.8 6.5 %collective-permute-start.4 = (bf16[2,1,16,4224]{3,2,1,0:T(8,128)(2,1)S(1)}, bf16[2,1,16,4224]{3,2,1,0:T(8,128)(2,1)S(1)}, u32[]{:S(2)}, u32[]{:S(2)}) collective-permute-start(bf16[2,1,16,4224]{3,2,1,0:T(8,128)(2,1)S(1)} %slice.40), channel_id=1, source_target_pairs={{0,1},{1,2},{2,3},{3,0},{4,5},{5,6},{6,7},{7,4},{8,9},{9,10},{10,1... | collective-permute-start | bytes 811016 | tf_op jit(solution)/shard_map/ppermute | solution.py:40
  28.6 7.7 %collective-permute-start.5 = (bf16[2,1,16,4224]{3,2,1,0:T(8,128)(2,1)S(1)}, bf16[2,1,16,4224]{3,2,1,0:T(8,128)(2,1)S(1)}, u32[]{:S(2)}, u32[]{:S(2)}) collective-permute-start(bf16[2,1,16,4224]{3,2,1,0:T(8,128)(2,1)S(1)} %slice.41), channel_id=1, source_target_pairs={{0,3},{1,0},{2,1},{3,2},{4,7},{5,4},{6,5},{7,6},{8,11},{9,8},{10,9... | collective-permute-start | bytes 811016 | tf_op jit(solution)/shard_map/ppermute | solution.py:40
  36.7 22.0 %collective-permute-start.12 = (bf16[256,4224]{1,0:T(8,128)(2,1)S(1)}, bf16[256,4224]{1,0:T(8,128)(2,1)S(1)}, u32[]{:S(2)}, u32[]{:S(2)}) collective-permute-start(bf16[256,4224]{1,0:T(8,128)(2,1)S(1)} %bitcast.58), channel_id=1, source_target_pairs={{0,32},{1,33},{2,34},{3,35},{4,36},{5,37},{6,38},{7,39},{8,40},{9,... | collective-permute-start | bytes 6488072 | tf_op jit(solution)/shard_map/ppermute | solution.py:40
  36.8 31.7 %collective-permute-start.7 = (bf16[256,4224]{1,0:T(8,128)(2,1)S(1)}, bf16[256,4224]{1,0:T(8,128)(2,1)S(1)}, u32[]{:S(2)}, u32[]{:S(2)}) collective-permute-start(bf16[256,4224]{1,0:T(8,128)(2,1)S(1)} %bitcast.59), channel_id=1, source_target_pairs={{0,24},{1,25},{2,26},{3,27},{4,28},{5,29},{6,30},{7,31},{8,0},{9,1... | collective-permute-start | bytes 6488072 | tf_op jit(solution)/shard_map/ppermute | solution.py:40
  39.9 32.3 %collective-permute-start.6 = (bf16[256,4224]{1,0:T(8,128)(2,1)S(1)}, bf16[256,4224]{1,0:T(8,128)(2,1)S(1)}, u32[]{:S(2)}, u32[]{:S(2)}) collective-permute-start(bf16[256,4224]{1,0:T(8,128)(2,1)S(1)} %bitcast.60), channel_id=1, source_target_pairs={{0,8},{1,9},{2,10},{3,11},{4,12},{5,13},{6,14},{7,15},{8,16},{9,17... | collective-permute-start | bytes 6488072 | tf_op jit(solution)/shard_map/ppermute | solution.py:40
  39.9 10.7 %collective-permute-start.8 = (bf16[1,2,16,4224]{3,2,1,0:T(8,128)(2,1)S(1)}, bf16[1,2,16,4224]{3,2,1,0:T(8,128)(2,1)S(1)}, u32[]{:S(2)}, u32[]{:S(2)}) collective-permute-start(bf16[1,2,16,4224]{3,2,1,0:T(8,128)(2,1)S(1)} %get-tuple-element.71), channel_id=1, source_target_pairs={{0,3},{1,0},{2,1},{3,2},{4,7},{5,4},{6,5},{7,6},{8,11},{9,8},{10,9... | collective-permute-start | bytes 811016 | tf_op jit(solution)/shard_map/ppermute | solution.py:40
  40.0 10.7 %collective-permute-start.9 = (bf16[1,2,16,4224]{3,2,1,0:T(8,128)(2,1)S(1)}, bf16[1,2,16,4224]{3,2,1,0:T(8,128)(2,1)S(1)}, u32[]{:S(2)}, u32[]{:S(2)}) collective-permute-start(bf16[1,2,16,4224]{3,2,1,0:T(8,128)(2,1)S(1)} %get-tuple-element.71), channel_id=1, source_target_pairs={{0,1},{1,2},{2,3},{3,0},{4,5},{5,6},{6,7},{7,4},{8,9},{9,10},{10,1... | collective-permute-start | bytes 811016 | tf_op jit(solution)/shard_map/ppermute | solution.py:40
  50.6 7.8 %collective-permute-start.11 = (bf16[1,1,16,4224]{3,2,1,0:T(8,128)(2,1)S(1)}, bf16[1,1,16,4224]{3,2,1,0:T(8,128)(2,1)S(1)}, u32[]{:S(2)}, u32[]{:S(2)}) collective-permute-start(bf16[1,1,16,4224]{3,2,1,0:T(8,128)(2,1)S(1)} %slice.51), channel_id=1, source_target_pairs={{0,3},{1,0},{2,1},{3,2},{4,7},{5,4},{6,5},{7,6},{8,11},{9,8},{10,9... | collective-permute-start | bytes 405512 | tf_op jit(solution)/shard_map/ppermute | solution.py:40
  50.7 7.7 %collective-permute-start.10 = (bf16[1,1,16,4224]{3,2,1,0:T(8,128)(2,1)S(1)}, bf16[1,1,16,4224]{3,2,1,0:T(8,128)(2,1)S(1)}, u32[]{:S(2)}, u32[]{:S(2)}) collective-permute-start(bf16[1,1,16,4224]{3,2,1,0:T(8,128)(2,1)S(1)} %slice.50), channel_id=1, source_target_pairs={{0,1},{1,2},{2,3},{3,0},{4,5},{5,6},{6,7},{7,4},{8,9},{9,10},{10,1... | collective-permute-start | bytes 405512 | tf_op jit(solution)/shard_map/ppermute | solution.py:40
  72.2 8.9 %collective-permute-start.13 = (bf16[256,4224]{1,0:T(8,128)(2,1)S(1)}, bf16[256,4224]{1,0:T(8,128)(2,1)S(1)}, u32[]{:S(2)}, u32[]{:S(2)}) collective-permute-start(bf16[256,4224]{1,0:T(8,128)(2,1)S(1)} %collective-permute-done.7.refs_0_.refs_13_), channel_id=1, source_target_pairs={{0,32},{1,33},{2,34},{3,35},{4,36},{5,37},{6,38},{7,39},{8,40},{9,... | collective-permute-start | bytes 6488072 | tf_op jit(solution)/shard_map/ppermute | solution.py:40
  72.2 8.9 %collective-permute-start.14 = (bf16[256,4224]{1,0:T(8,128)(2,1)S(1)}, bf16[256,4224]{1,0:T(8,128)(2,1)S(1)}, u32[]{:S(2)}, u32[]{:S(2)}) collective-permute-start(bf16[256,4224]{1,0:T(8,128)(2,1)S(1)} %collective-permute-done.6.refs_1_.refs_14_), channel_id=1, source_target_pairs={{0,32},{1,33},{2,34},{3,35},{4,36},{5,37},{6,38},{7,39},{8,40},{9,... | collective-permute-start | bytes 6488072 | tf_op jit(solution)/shard_map/ppermute | solution.py:40
  72.7 8.4 %collective-permute-start.15 = (bf16[128,4224]{1,0:T(8,128)(2,1)S(1)}, bf16[128,4224]{1,0:T(8,128)(2,1)S(1)}, u32[]{:S(2)}, u32[]{:S(2)}) collective-permute-start(bf16[128,4224]{1,0:T(8,128)(2,1)S(1)} %bitcast.63), channel_id=1, source_target_pairs={{0,32},{1,33},{2,34},{3,35},{4,36},{5,37},{6,38},{7,39},{8,40},{9,... | collective-permute-start | bytes 3244040 | tf_op jit(solution)/shard_map/ppermute | solution.py:40
  72.7 16.4 %collective-permute-start.20 = (bf16[128,4224]{1,0:T(8,128)(2,1)S(1)}, bf16[128,4224]{1,0:T(8,128)(2,1)S(1)}, u32[]{:S(2)}, u32[]{:S(2)}) collective-permute-start(bf16[128,4224]{1,0:T(8,128)(2,1)S(1)} %slice.46), channel_id=1, source_target_pairs={{0,8},{1,9},{2,10},{3,11},{4,12},{5,13},{6,14},{7,15},{8,16},{9,17... | collective-permute-start | bytes 3244040 | tf_op jit(solution)/shard_map/ppermute | solution.py:40
  72.9 16.3 %collective-permute-start.21 = (bf16[128,4224]{1,0:T(8,128)(2,1)S(1)}, bf16[128,4224]{1,0:T(8,128)(2,1)S(1)}, u32[]{:S(2)}, u32[]{:S(2)}) collective-permute-start(bf16[128,4224]{1,0:T(8,128)(2,1)S(1)} %slice.47), channel_id=1, source_target_pairs={{0,24},{1,25},{2,26},{3,27},{4,28},{5,29},{6,30},{7,31},{8,0},{9,1... | collective-permute-start | bytes 3244040 | tf_op jit(solution)/shard_map/ppermute | solution.py:40
  81.1 19.4 %collective-permute-start.17 = (bf16[128,4224]{1,0:T(8,128)(2,1)S(1)}, bf16[128,4224]{1,0:T(8,128)(2,1)S(1)}, u32[]{:S(2)}, u32[]{:S(2)}) collective-permute-start(bf16[128,4224]{1,0:T(8,128)(2,1)S(1)} %bitcast.64), channel_id=1, source_target_pairs={{0,24},{1,25},{2,26},{3,27},{4,28},{5,29},{6,30},{7,31},{8,0},{9,1... | collective-permute-start | bytes 3244040 | tf_op jit(solution)/shard_map/ppermute | solution.py:40
  81.2 19.5 %collective-permute-start.16 = (bf16[128,4224]{1,0:T(8,128)(2,1)S(1)}, bf16[128,4224]{1,0:T(8,128)(2,1)S(1)}, u32[]{:S(2)}, u32[]{:S(2)}) collective-permute-start(bf16[128,4224]{1,0:T(8,128)(2,1)S(1)} %bitcast.65), channel_id=1, source_target_pairs={{0,8},{1,9},{2,10},{3,11},{4,12},{5,13},{6,14},{7,15},{8,16},{9,17... | collective-permute-start | bytes 3244040 | tf_op jit(solution)/shard_map/ppermute | solution.py:40
  89.2 15.7 %collective-permute-start.22 = (bf16[128,4224]{1,0:T(8,128)(2,1)S(1)}, bf16[128,4224]{1,0:T(8,128)(2,1)S(1)}, u32[]{:S(2)}, u32[]{:S(2)}) collective-permute-start(bf16[128,4224]{1,0:T(8,128)(2,1)S(1)} %collective-permute-done.20.refs_0_.refs_19_), channel_id=1, source_target_pairs={{0,32},{1,33},{2,34},{3,35},{4,36},{5,37},{6,38},{7,39},{8,40},{9,... | collective-permute-start | bytes 3244040 | tf_op jit(solution)/shard_map/ppermute | solution.py:40
  89.2 15.7 %collective-permute-start.23 = (bf16[128,4224]{1,0:T(8,128)(2,1)S(1)}, bf16[128,4224]{1,0:T(8,128)(2,1)S(1)}, u32[]{:S(2)}, u32[]{:S(2)}) collective-permute-start(bf16[128,4224]{1,0:T(8,128)(2,1)S(1)} %collective-permute-done.21.refs_1_.refs_20_), channel_id=1, source_target_pairs={{0,32},{1,33},{2,34},{3,35},{4,36},{5,37},{6,38},{7,39},{8,40},{9,... | collective-permute-start | bytes 3244040 | tf_op jit(solution)/shard_map/ppermute | solution.py:40
  100.8 4.2 %collective-permute-start.25 = (bf16[128,4224]{1,0:T(8,128)(2,1)S(1)}, bf16[128,4224]{1,0:T(8,128)(2,1)S(1)}, u32[]{:S(2)}, u32[]{:S(2)}) collective-permute-start(bf16[128,4224]{1,0:T(8,128)(2,1)S(1)} %collective-permute-done.16.refs_3_.refs_22_), channel_id=1, source_target_pairs={{0,32},{1,33},{2,34},{3,35},{4,36},{5,37},{6,38},{7,39},{8,40},{9,... | collective-permute-start | bytes 3244040 | tf_op jit(solution)/shard_map/ppermute | solution.py:40
  100.8 4.3 %collective-permute-start.24 = (bf16[128,4224]{1,0:T(8,128)(2,1)S(1)}, bf16[128,4224]{1,0:T(8,128)(2,1)S(1)}, u32[]{:S(2)}, u32[]{:S(2)}) collective-permute-start(bf16[128,4224]{1,0:T(8,128)(2,1)S(1)} %collective-permute-done.17.refs_2_.refs_21_), channel_id=1, source_target_pairs={{0,32},{1,33},{2,34},{3,35},{4,36},{5,37},{6,38},{7,39},{8,40},{9,... | collective-permute-start | bytes 3244040 | tf_op jit(solution)/shard_map/ppermute | solution.py:40
  101.4 10.6 %collective-permute-start.19 = (bf16[64,4224]{1,0:T(8,128)(2,1)S(1)}, bf16[64,4224]{1,0:T(8,128)(2,1)S(1)}, u32[]{:S(2)}, u32[]{:S(2)}) collective-permute-start(bf16[64,4224]{1,0:T(8,128)(2,1)S(1)} %slice.45), channel_id=1, source_target_pairs={{0,24},{1,25},{2,26},{3,27},{4,28},{5,29},{6,30},{7,31},{8,0},{9,1... | collective-permute-start | bytes 1622024 | tf_op jit(solution)/shard_map/ppermute | solution.py:40
  104.9 10.6 %collective-permute-start.18 = (bf16[64,4224]{1,0:T(8,128)(2,1)S(1)}, bf16[64,4224]{1,0:T(8,128)(2,1)S(1)}, u32[]{:S(2)}, u32[]{:S(2)}) collective-permute-start(bf16[64,4224]{1,0:T(8,128)(2,1)S(1)} %slice.44), channel_id=1, source_target_pairs={{0,8},{1,9},{2,10},{3,11},{4,12},{5,13},{6,14},{7,15},{8,16},{9,17... | collective-permute-start | bytes 1622024 | tf_op jit(solution)/shard_map/ppermute | solution.py:40
  131.1 5.0 %collective-permute-start.30 = (f32[24,128]{1,0:T(8,128)S(1)}, f32[24,128]{1,0:T(8,128)S(1)}, u32[]{:S(2)}, u32[]{:S(2)}) collective-permute-start(f32[24,128]{1,0:T(8,128)S(1)} %log_add_fusion.5), channel_id=1, source_target_pairs={{0,68},{1,69},{2,70},{3,71},{4,64},{5,65},{6,66},{7,67},{8,76},{9,... | collective-permute-start | bytes 36872 | tf_op jit(solution)/shard_map/ppermute | solution.py:40
  140.2 5.0 %collective-permute-start.32 = (f32[24,128]{1,0:T(8,128)S(1)}, f32[24,128]{1,0:T(8,128)S(1)}, u32[]{:S(2)}, u32[]{:S(2)}) collective-permute-start(f32[24,128]{1,0:T(8,128)S(1)} %log_add_fusion.3), channel_id=1, source_target_pairs={{0,3},{1,2},{2,1},{3,0},{4,7},{5,6},{6,5},{7,4},{8,11},{9,10},{10,... | collective-permute-start | bytes 36872 | tf_op jit(solution)/shard_map/ppermute | solution.py:40
  149.0 5.0 %collective-permute-start.34 = (f32[24,128]{1,0:T(8,128)S(1)}, f32[24,128]{1,0:T(8,128)S(1)}, u32[]{:S(2)}, u32[]{:S(2)}) collective-permute-start(f32[24,128]{1,0:T(8,128)S(1)} %log_add_fusion.1), channel_id=1, source_target_pairs={{0,24},{1,25},{2,26},{3,27},{4,28},{5,29},{6,30},{7,31},{8,16},{9,... | collective-permute-start | bytes 36872 | tf_op jit(solution)/shard_map/ppermute | solution.py:40
  186.4 5.0 %collective-permute-start.37 = (f32[1,4096]{1,0:T(1,128)S(1)}, f32[1,4096]{1,0:T(1,128)S(1)}, u32[]{:S(2)}, u32[]{:S(2)}) collective-permute-start(f32[1,4096]{1,0:T(1,128)S(1)} %add.135), channel_id=1, source_target_pairs={{0,68},{1,69},{2,70},{3,71},{4,64},{5,65},{6,66},{7,67},{8,76},{9,... | collective-permute-start | bytes 49160 | tf_op jit(solution)/shard_map/ppermute | solution.py:40
  195.3 5.0 %collective-permute-start.39 = (f32[1,4096]{1,0:T(1,128)S(1)}, f32[1,4096]{1,0:T(1,128)S(1)}, u32[]{:S(2)}, u32[]{:S(2)}) collective-permute-start(f32[1,4096]{1,0:T(1,128)S(1)} %add.137), channel_id=1, source_target_pairs={{0,3},{1,2},{2,1},{3,0},{4,7},{5,6},{6,5},{7,4},{8,11},{9,10},{10,... | collective-permute-start | bytes 49160 | tf_op jit(solution)/shard_map/ppermute | solution.py:40
  204.2 5.0 %collective-permute-start.41 = (f32[1,4096]{1,0:T(1,128)S(1)}, f32[1,4096]{1,0:T(1,128)S(1)}, u32[]{:S(2)}, u32[]{:S(2)}) collective-permute-start(f32[1,4096]{1,0:T(1,128)S(1)} %add.139), channel_id=1, source_target_pairs={{0,24},{1,25},{2,26},{3,27},{4,28},{5,29},{6,30},{7,31},{8,16},{9,... | collective-permute-start | bytes 49160 | tf_op jit(solution)/shard_map/ppermute | solution.py:40
  (42 other events, 417.8 us)

commit v2 on v1

--- a/solution.py
+++ b/solution.py
@@ -20,7 +20,7 @@
 SETS = (2, 1)
 CALLS = (((0, 0),), ((0, 1), (0, 3), (1, 0)), ((0, 2), (1, 1), (1, 3)), ((1, 2),))
 TILE = 256
-DBLOCK = 512
+DBLOCK = 1024
 PART = 256
 FORWARD_LIMIT = 16 * 1024 * 1024
 VMEM_LIMIT = 60 * 1024 * 1024
@@ -76,6 +76,40 @@
 def slab_of(two, right, far, left):
     groups, _, _, width = two.shape
     return jnp.stack([two, right, far, left], axis=1).reshape(groups * LANES, width)
+
+
+def normalize_kernel(place_ref, labels_ref, hidden_ref, gain_ref, *out_refs):
+    core = place_ref[0]
+    _, rows, features = hidden_ref.shape
+    wide = hidden_ref[core].astype(jnp.float32)
+    factor = lax.rsqrt(jnp.mean(wide * wide, axis=-1, keepdims=True) + EPS)
+    scaled = (wide * factor * gain_ref[...].astype(jnp.float32)).astype(jnp.bfloat16)
+    row = lax.broadcasted_iota(jnp.int32, (rows, LANES), 0)
+    lane = lax.broadcasted_iota(jnp.int32, (rows, LANES), 1)
+    label = jnp.zeros((rows, LANES), jnp.int32)
+    for k in range(rows):
+        label = jnp.where(row == k, labels_ref[core, k], label)
+    codes = jnp.where(lane == 0, label // 256, jnp.where(lane == 1, label % 256, 0))
+    codes = codes.astype(jnp.float32).astype(jnp.bfloat16)
+    at = 0
+    for out_ref in out_refs:
+        held = slice(at, at + out_ref.shape[0])
+        out_ref[:, :features] = scaled[held]
+        out_ref[:, features:] = codes[held]
+        at += out_ref.shape[0]
+
+
+def normalized(place, labels, hidden, gain):
+    _, _, features = hidden.shape
+    smem, vmem = pl.BlockSpec(memory_space=pltpu.SMEM), pl.BlockSpec(memory_space=pltpu.VMEM)
+    sets = pl.pallas_call(
+        normalize_kernel,
+        out_shape=[jax.ShapeDtypeStruct((groups * ROWS, features + LANES), jnp.bfloat16) for groups in SETS],
+        in_specs=[smem, smem, vmem, vmem],
+        out_specs=[vmem] * len(SETS),
+        name="normalized",
+    )(place, labels, hidden, gain[None])
+    return [rows.reshape(groups, ROWS, features + LANES) for rows, groups in zip(sets, SETS)]
 
 
 def forward_kernel(features, sizes, wt_ref, *refs):
@@ -317,22 +351,16 @@
     place = jnp.stack([core, lax.axis_index("y"), lax.axis_index("zh"), lax.axis_index("x")]).astype(jnp.int32)
     base = (lax.axis_index(VOCAB_FSDP) * columns).astype(jnp.int32).reshape(1)
     gain_wide = norm_gain.astype(jnp.float32)
-    wide = lax.dynamic_index_in_dim(hidden, core, 0, keepdims=False).astype(jnp.float32)
-    factor = lax.rsqrt(jnp.mean(wide * wide, axis=-1, keepdims=True) + EPS)
-    scaled = (wide * factor * gain_wide).astype(jnp.bfloat16)
-    own_labels = lax.dynamic_index_in_dim(labels, core, 0, keepdims=False)[:, None]
-    lane = lax.broadcasted_iota(jnp.int32, (own_rows, LANES), 1)
-    codes = jnp.where(lane == 0, own_labels // 256, jnp.where(lane == 1, own_labels % 256, 0)).astype(jnp.bfloat16)
-    own = jnp.concatenate([scaled, codes], axis=1).reshape(own_rows // ROWS, ROWS, features + LANES)
+    own0, own1 = normalized(place, labels, hidden, norm_gain)
     count = batches * own_rows * 32
     wt = head_weight.T
 
     tie = lax.optimization_barrier
-    own0, own1 = own[: SETS[0]], own[SETS[0] :]
     z0, z1 = z_swap(own0), z_swap(own1)
+    z0, wt = tie((z0, wt))
     two0 = jnp.stack([own0, z0], axis=1)
     left0, right0 = shift(two0, 1, 0), shift(two0, -1, 0)
-    left0, right0, z1, wt = tie((left0, right0, z1, wt))
+    left0, right0, z1 = tie((left0, right0, z1))
     two1 = jnp.stack([own1, z1], axis=1)
     far0 = [shift(left0[:, :1], 1, 0), shift(right0[:, 1:], -1, 0)]
     left1, right1 = shift(two1, 1, 0), shift(two1, -1, 0)

time: 210 us -> 206 us (0.981)
  starting transfers between devices: 35.9 us -> 40.6 us
  other arithmetic: 8.1 us -> 4.23 us
  waiting for transfers between devices: 106 us -> 103 us
  local copies, waits for them, and re-layouts: 15.3 us -> 12.5 us
    ppermute x42, starting transfers between devices: 35.9 us -> 40.6 us  [moved(): return lax.ppermute(value, AXES, pairs)]
    unnamed x65 -> x67, local copies, waits for them, and re-layouts: 15 us -> 10.9 us
    ppermute x42, waiting for transfers between devices: 106 us -> 103 us  [moved(): return lax.ppermute(value, AXES, pairs)]
    pallas_call x0 -> x1, Pallas kernels: none -> 2.17 us  [normalized(): pl.pallas_call(normalize_kernel, out_shape=[jax.ShapeDtypeStruct((groups...]
  transfers between devices with their start and end apart: 42 -> 42, of which waited for: 29 -> 33; matrix products, arithmetic and copies ran while one was open for 4% -> 3% of each run, Pallas kernels for 7% -> 7%
where the time goes in v2:
time: 206 us; the launch traced here: 205 us
  waiting for transfers between devices  103 us (50%)
  Pallas kernels  44.2 us (21%)
  starting transfers between devices  40.6 us (20%)
  local copies, waits for them, and re-layouts  12.5 us (6%)
  other arithmetic  4.23 us (2%)
    ppermute x42, waiting for transfers between devices, moved(): return lax.ppermute(value, AXES, pairs)  103 us
    ppermute x42, starting transfers between devices, moved(): return lax.ppermute(value, AXES, pairs)  40.6 us
    pallas_call x1, Pallas kernels, backward(): pl.pallas_call(functools.partial(backward_kernel, sizes, widths, count),...  24.9 us
    pallas_call x4, Pallas kernels, forward(): pl.pallas_call(functools.partial(forward_kernel, features, sizes), out_sh...  15.2 us
    unnamed x67, local copies, waits for them, and re-layouts  10.9 us
  transfers between devices with their start and end apart: 42, of which 33 were waited for; matrix products, arithmetic and copies ran while one was open for 3% of the time, Pallas kernels for 7%

profile of v2, /device:TPU:6, one launch (start us, length us, event | category | flops | bytes accessed | tf_op | source)
XLA Modules:
  0.0 205.4 jit_solution(9577253982725894114)
XLA Ops:
  4.8 4.1 %collective-permute-start = (bf16[2,16,4224]{2,1,0:T(8,128)(2,1)}, bf16[2,16,4224]{2,1,0:T(8,128)(2,1)S(1)}, u32[]{:S(2)}, u32[]{:S(2)}) collective-permute-start(bf16[2,16,4224]{2,1,0:T(8,128)(2,1)} %bitcast.54), channel_id=1, source_target_pairs={{0,68},{1,69},{2,70},{3,71},{4,64},{5,65},{6,66},{7,67},{8,76},{9,... | collective-permute-start | bytes 811016 | tf_op jit(solution)/shard_map/ppermute | solution.py:40
  8.9 6.4 %copy.8 = bf16[4096,512]{0,1:T(8,128)(2,1)} copy(bf16[4096,512]{1,0:T(8,128)(2,1)} %param.9) | data formatting | bytes 8388608 | tf_op args[3]
  17.8 2.9 %collective-permute-start.3 = (bf16[1,16,4224]{2,1,0:T(8,128)(2,1)S(1)}, bf16[1,16,4224]{2,1,0:T(8,128)(2,1)S(1)}, u32[]{:S(2)}, u32[]{:S(2)}) collective-permute-start(bf16[1,16,4224]{2,1,0:T(8,128)(2,1)S(1)} %bitcast.57), channel_id=1, source_target_pairs={{0,68},{1,69},{2,70},{3,71},{4,64},{5,65},{6,66},{7,67},{8,76},{9,... | collective-permute-start | bytes 405512 | tf_op jit(solution)/shard_map/ppermute | solution.py:40
  20.7 3.8 %collective-permute-done.3 = bf16[1,16,4224]{2,1,0:T(8,128)(2,1)S(1)} collective-permute-done((bf16[1,16,4224]{2,1,0:T(8,128)(2,1)S(1)}, bf16[1,16,4224]{2,1,0:T(8,128)(2,1)S(1)}, u32[]{:S(2)}, u32[]{:S(2)}) %collective-permute-start.3) | collective-permute-done | bytes 135200 | tf_op jit(solution)/shard_map/ppermute | solution.py:40
  28.9 4.4 %collective-permute-done.4 = bf16[2,1,16,4224]{3,2,1,0:T(8,128)(2,1)S(1)} collective-permute-done((bf16[2,1,16,4224]{3,2,1,0:T(8,128)(2,1)S(1)}, bf16[2,1,16,4224]{3,2,1,0:T(8,128)(2,1)S(1)}, u32[]{:S(2)}, u32[]{:S(2)}) %collective-permute-start.4) | collective-permute-done | bytes 270368 | tf_op jit(solution)/shard_map/ppermute | solution.py:40
  35.3 3.1 %collective-permute-start.7 = (bf16[256,4224]{1,0:T(8,128)(2,1)S(1)}, bf16[256,4224]{1,0:T(8,128)(2,1)S(1)}, u32[]{:S(2)}, u32[]{:S(2)}) collective-permute-start(bf16[256,4224]{1,0:T(8,128)(2,1)S(1)} %bitcast.41), channel_id=1, source_target_pairs={{0,24},{1,25},{2,26},{3,27},{4,28},{5,29},{6,30},{7,31},{8,0},{9,1... | collective-permute-start | bytes 6488072 | tf_op jit(solution)/shard_map/ppermute | solution.py:40
  41.8 7.4 %collective-permute-done.8 = bf16[1,2,16,4224]{3,2,1,0:T(8,128)(2,1)S(1)} collective-permute-done((bf16[1,2,16,4224]{3,2,1,0:T(8,128)(2,1)S(1)}, bf16[1,2,16,4224]{3,2,1,0:T(8,128)(2,1)S(1)}, u32[]{:S(2)}, u32[]{:S(2)}) %collective-permute-start.8) | collective-permute-done | bytes 270368 | tf_op jit(solution)/shard_map/ppermute | solution.py:40
  49.3 3.3 %collective-permute-start.10 = (bf16[1,1,16,4224]{3,2,1,0:T(8,128)(2,1)S(1)}, bf16[1,1,16,4224]{3,2,1,0:T(8,128)(2,1)S(1)}, u32[]{:S(2)}, u32[]{:S(2)}) collective-permute-start(bf16[1,1,16,4224]{3,2,1,0:T(8,128)(2,1)S(1)} %slice.32), channel_id=1, source_target_pairs={{0,1},{1,2},{2,3},{3,0},{4,5},{5,6},{6,7},{7,4},{8,9},{9,10},{10,1... | collective-permute-start | bytes 405512 | tf_op jit(solution)/shard_map/ppermute | solution.py:40
  52.6 4.4 %collective-permute-done.11 = bf16[1,1,16,4224]{3,2,1,0:T(8,128)(2,1)S(1)} collective-permute-done((bf16[1,1,16,4224]{3,2,1,0:T(8,128)(2,1)S(1)}, bf16[1,1,16,4224]{3,2,1,0:T(8,128)(2,1)S(1)}, u32[]{:S(2)}, u32[]{:S(2)}) %collective-permute-start.11) | collective-permute-done | bytes 135200 | tf_op jit(solution)/shard_map/ppermute | solution.py:40
  61.4 5.6 %collective-permute-done.7.refs_0_.refs_13_ = bf16[256,4224]{1,0:T(8,128)(2,1)S(1)} collective-permute-done((bf16[256,4224]{1,0:T(8,128)(2,1)S(1)}, bf16[256,4224]{1,0:T(8,128)(2,1)S(1)}, u32[]{:S(2)}, u32[]{:S(2)}) %collective-permute-start.7) | collective-permute-done | bytes 2162720 | tf_op jit(solution)/shard_map/ppermute | solution.py:40
  67.0 3.7 %collective-permute-done.6.refs_1_.refs_14_ = bf16[256,4224]{1,0:T(8,128)(2,1)S(1)} collective-permute-done((bf16[256,4224]{1,0:T(8,128)(2,1)S(1)}, bf16[256,4224]{1,0:T(8,128)(2,1)S(1)}, u32[]{:S(2)}, u32[]{:S(2)}) %collective-permute-start.6) | collective-permute-done | bytes 2162720 | tf_op jit(solution)/shard_map/ppermute | solution.py:40
  71.5 3.3 %collective-permute-start.21 = (bf16[128,4224]{1,0:T(8,128)(2,1)S(1)}, bf16[128,4224]{1,0:T(8,128)(2,1)S(1)}, u32[]{:S(2)}, u32[]{:S(2)}) collective-permute-start(bf16[128,4224]{1,0:T(8,128)(2,1)S(1)} %slice.31), channel_id=1, source_target_pairs={{0,24},{1,25},{2,26},{3,27},{4,28},{5,29},{6,30},{7,31},{8,0},{9,1... | collective-permute-start | bytes 3244040 | tf_op jit(solution)/shard_map/ppermute | solution.py:40
  74.8 4.8 %collective-permute-done.15.refs_5_.refs_18_ = bf16[128,4224]{1,0:T(8,128)(2,1)S(1)} collective-permute-done((bf16[128,4224]{1,0:T(8,128)(2,1)S(1)}, bf16[128,4224]{1,0:T(8,128)(2,1)S(1)}, u32[]{:S(2)}, u32[]{:S(2)}) %collective-permute-start.15) | collective-permute-done | bytes 1081376 | tf_op jit(solution)/shard_map/ppermute | solution.py:40
  81.7 6.0 %collective-permute-done.20.refs_0_.refs_19_ = bf16[128,4224]{1,0:T(8,128)(2,1)S(1)} collective-permute-done((bf16[128,4224]{1,0:T(8,128)(2,1)S(1)}, bf16[128,4224]{1,0:T(8,128)(2,1)S(1)}, u32[]{:S(2)}, u32[]{:S(2)}) %collective-permute-start.20) | collective-permute-done | bytes 1081376 | tf_op jit(solution)/shard_map/ppermute | solution.py:40
  88.3 6.2 %forward.5 = (f32[512,1280]{1,0:T(8,128)S(1)}, f32[3,10,128]{2,1,0:T(8,128)S(1)}) custom-call(bf16[512,4096]{1,0:T(8,128)(2,1)S(1)} %bitcast.37, bf16[256,4224]{1,0:T(8,128)(2,1)S(1)} %collective-permute-done.7.refs_0_.refs_13_, bf16[256,4224]{1,0:T(8,128)(2,1)S(1)} %collective-permute-done.6.refs_1_.refs_14_, bf16[128,4224]{1,0:T(8,128)(2,1)S(1)} %bitcast.48, ...), custom_call_target="tpu_custom_call" | custom-call | flops 5368709120 | bytes 17629184 | tf_op jit(solution)/shard_map/forward/pallas_call | solution.py:159
  96.0 3.1 %collective-permute-done.17.refs_2_.refs_21_ = bf16[128,4224]{1,0:T(8,128)(2,1)S(1)} collective-permute-done((bf16[128,4224]{1,0:T(8,128)(2,1)S(1)}, bf16[128,4224]{1,0:T(8,128)(2,1)S(1)}, u32[]{:S(2)}, u32[]{:S(2)}) %collective-permute-start.17) | collective-permute-done | bytes 1081376 | tf_op jit(solution)/shard_map/ppermute | solution.py:40
  99.9 3.5 %collective-permute-start.19 = (bf16[64,4224]{1,0:T(8,128)(2,1)S(1)}, bf16[64,4224]{1,0:T(8,128)(2,1)S(1)}, u32[]{:S(2)}, u32[]{:S(2)}) collective-permute-start(bf16[64,4224]{1,0:T(8,128)(2,1)S(1)} %slice.29), channel_id=1, source_target_pairs={{0,24},{1,25},{2,26},{3,27},{4,28},{5,29},{6,30},{7,31},{8,0},{9,1... | collective-permute-start | bytes 1622024 | tf_op jit(solution)/shard_map/ppermute | solution.py:40
  103.6 5.0 %forward.6 = (f32[512,1024]{1,0:T(8,128)S(1)}, f32[3,8,128]{2,1,0:T(8,128)S(1)}) custom-call(bf16[512,4096]{1,0:T(8,128)(2,1)S(1)} %bitcast.38, bf16[128,4224]{1,0:T(8,128)(2,1)S(1)} %collective-permute-done.20.refs_0_.refs_19_, bf16[128,4224]{1,0:T(8,128)(2,1)S(1)} %collective-permute-done.21.refs_1_.refs_20_, ...), custom_call_target="tpu_custom_call" | custom-call | flops 4294967296 | bytes 14942208 | tf_op jit(solution)/shard_map/forward/pallas_call | solution.py:159
  110.3 3.7 %collective-permute-done.18.refs_0_.refs_27_ = bf16[64,4224]{1,0:T(8,128)(2,1)S(1)} collective-permute-done((bf16[64,4224]{1,0:T(8,128)(2,1)S(1)}, bf16[64,4224]{1,0:T(8,128)(2,1)S(1)}, u32[]{:S(2)}, u32[]{:S(2)}) %collective-permute-start.18) | collective-permute-done | bytes 540704 | tf_op jit(solution)/shard_map/ppermute | solution.py:40
  123.9 3.7 %collective-permute-done.29 = f32[24,128]{1,0:T(8,128)S(1)} collective-permute-done((f32[24,128]{1,0:T(8,128)S(1)}, f32[24,128]{1,0:T(8,128)S(1)}, u32[]{:S(2)}, u32[]{:S(2)}) %collective-permute-start.29) | collective-permute-done | bytes 12320 | tf_op jit(solution)/shard_map/ppermute | solution.py:40
  127.6 3.0 %collective-permute-start.30 = (f32[24,128]{1,0:T(8,128)S(1)}, f32[24,128]{1,0:T(8,128)S(1)}, u32[]{:S(2)}, u32[]{:S(2)}) collective-permute-start(f32[24,128]{1,0:T(8,128)S(1)} %log_add_fusion.5), channel_id=1, source_target_pairs={{0,68},{1,69},{2,70},{3,71},{4,64},{5,65},{6,66},{7,67},{8,76},{9,... | collective-permute-start | bytes 36872 | tf_op jit(solution)/shard_map/ppermute | solution.py:40
  133.4 3.2 %collective-permute-done.31 = f32[24,128]{1,0:T(8,128)S(1)} collective-permute-done((f32[24,128]{1,0:T(8,128)S(1)}, f32[24,128]{1,0:T(8,128)S(1)}, u32[]{:S(2)}, u32[]{:S(2)}) %collective-permute-start.31) | collective-permute-done | bytes 12320 | tf_op jit(solution)/shard_map/ppermute | solution.py:40
  136.9 4.6 %collective-permute-done.32 = f32[24,128]{1,0:T(8,128)S(1)} collective-permute-done((f32[24,128]{1,0:T(8,128)S(1)}, f32[24,128]{1,0:T(8,128)S(1)}, u32[]{:S(2)}, u32[]{:S(2)}) %collective-permute-start.32) | collective-permute-done | bytes 12320 | tf_op jit(solution)/shard_map/ppermute | solution.py:40
  141.7 3.7 %collective-permute-done.33 = f32[24,128]{1,0:T(8,128)S(1)} collective-permute-done((f32[24,128]{1,0:T(8,128)S(1)}, f32[24,128]{1,0:T(8,128)S(1)}, u32[]{:S(2)}, u32[]{:S(2)}) %collective-permute-start.33) | collective-permute-done | bytes 12320 | tf_op jit(solution)/shard_map/ppermute | solution.py:40
  145.5 4.8 %collective-permute-done.34 = f32[24,128]{1,0:T(8,128)S(1)} collective-permute-done((f32[24,128]{1,0:T(8,128)S(1)}, f32[24,128]{1,0:T(8,128)S(1)}, u32[]{:S(2)}, u32[]{:S(2)}) %collective-permute-start.34) | collective-permute-done | bytes 12320 | tf_op jit(solution)/shard_map/ppermute | solution.py:40
  151.0 24.9 %backward.1 = (f32[4096,512]{1,0:T(8,128)}, f32[1,4096]{1,0:T(1,128)}) custom-call(s32[4]{0:T(128)} %pad_add_fusion.place_ref, s32[1]{0:T(128)} %bitcast.4.base_ref, f32[3,4,128]{2,1,0:T(4,128)} %copy-done.14, f32[3,10,128]{2,1,0:T(8,128)} %copy-done.12, f32[3,8,128]{2,1,0:T(8,128)} %copy-done.13, f32[3,2,128]{2,1,0:T(2,128)} %copy-done.15, ...), custom_call_target="tpu_custom_call" | custom-call | flops 12884901888 | bytes 52428800 | tf_op jit(solution)/shard_map/backward/pallas_call | solution.py:308
  178.2 3.7 %collective-permute-done.36 = f32[1,4096]{1,0:T(1,128)S(1)} collective-permute-done((f32[1,4096]{1,0:T(1,128)S(1)}, f32[1,4096]{1,0:T(1,128)S(1)}, u32[]{:S(2)}, u32[]{:S(2)}) %collective-permute-start.36) | collective-permute-done | bytes 16416 | tf_op jit(solution)/shard_map/ppermute | solution.py:40
  181.9 3.0 %collective-permute-start.37 = (f32[1,4096]{1,0:T(1,128)S(1)}, f32[1,4096]{1,0:T(1,128)S(1)}, u32[]{:S(2)}, u32[]{:S(2)}) collective-permute-start(f32[1,4096]{1,0:T(1,128)S(1)} %add.97), channel_id=1, source_target_pairs={{0,68},{1,69},{2,70},{3,71},{4,64},{5,65},{6,66},{7,67},{8,76},{9,... | collective-permute-start | bytes 49160 | tf_op jit(solution)/shard_map/ppermute | solution.py:40
  187.1 3.7 %collective-permute-done.38 = f32[1,4096]{1,0:T(1,128)S(1)} collective-permute-done((f32[1,4096]{1,0:T(1,128)S(1)}, f32[1,4096]{1,0:T(1,128)S(1)}, u32[]{:S(2)}, u32[]{:S(2)}) %collective-permute-start.38) | collective-permute-done | bytes 16416 | tf_op jit(solution)/shard_map/ppermute | solution.py:40
  191.2 4.7 %collective-permute-done.39 = f32[1,4096]{1,0:T(1,128)S(1)} collective-permute-done((f32[1,4096]{1,0:T(1,128)S(1)}, f32[1,4096]{1,0:T(1,128)S(1)}, u32[]{:S(2)}, u32[]{:S(2)}) %collective-permute-start.39) | collective-permute-done | bytes 16416 | tf_op jit(solution)/shard_map/ppermute | solution.py:40
  196.0 3.7 %collective-permute-done.40 = f32[1,4096]{1,0:T(1,128)S(1)} collective-permute-done((f32[1,4096]{1,0:T(1,128)S(1)}, f32[1,4096]{1,0:T(1,128)S(1)}, u32[]{:S(2)}, u32[]{:S(2)}) %collective-permute-start.40) | collective-permute-done | bytes 16416 | tf_op jit(solution)/shard_map/ppermute | solution.py:40
  199.9 4.9 %collective-permute-done.41 = f32[1,4096]{1,0:T(1,128)S(1)} collective-permute-done((f32[1,4096]{1,0:T(1,128)S(1)}, f32[1,4096]{1,0:T(1,128)S(1)}, u32[]{:S(2)}, u32[]{:S(2)}) %collective-permute-start.41) | collective-permute-done | bytes 16416 | tf_op jit(solution)/shard_map/ppermute | solution.py:40
  (157 shorter events, 47.9 us)
Async XLA Ops:
  4.8 10.8 %collective-permute-start = (bf16[2,16,4224]{2,1,0:T(8,128)(2,1)}, bf16[2,16,4224]{2,1,0:T(8,128)(2,1)S(1)}, u32[]{:S(2)}, u32[]{:S(2)}) collective-permute-start(bf16[2,16,4224]{2,1,0:T(8,128)(2,1)} %bitcast.54), channel_id=1, source_target_pairs={{0,68},{1,69},{2,70},{3,71},{4,64},{5,65},{6,66},{7,67},{8,76},{9,... | collective-permute-start | bytes 811016 | tf_op jit(solution)/shard_map/ppermute | solution.py:40
  15.7 9.4 %collective-permute-start.1 = (bf16[2,2,16,4224]{3,2,1,0:T(8,128)(2,1)S(1)}, bf16[2,2,16,4224]{3,2,1,0:T(8,128)(2,1)S(1)}, u32[]{:S(2)}, u32[]{:S(2)}) collective-permute-start(bf16[2,2,16,4224]{3,2,1,0:T(8,128)(2,1)S(1)} %get-tuple-element.71), channel_id=1, source_target_pairs={{0,1},{1,2},{2,3},{3,0},{4,5},{5,6},{6,7},{7,4},{8,9},{9,10},{10,1... | collective-permute-start | bytes 1622024 | tf_op jit(solution)/shard_map/ppermute | solution.py:40
  16.2 10.6 %collective-permute-start.2 = (bf16[2,2,16,4224]{3,2,1,0:T(8,128)(2,1)S(1)}, bf16[2,2,16,4224]{3,2,1,0:T(8,128)(2,1)S(1)}, u32[]{:S(2)}, u32[]{:S(2)}) collective-permute-start(bf16[2,2,16,4224]{3,2,1,0:T(8,128)(2,1)S(1)} %get-tuple-element.71), channel_id=1, source_target_pairs={{0,3},{1,0},{2,1},{3,2},{4,7},{5,4},{6,5},{7,6},{8,11},{9,8},{10,9... | collective-permute-start | bytes 1622024 | tf_op jit(solution)/shard_map/ppermute | solution.py:40
  17.8 6.8 %collective-permute-start.3 = (bf16[1,16,4224]{2,1,0:T(8,128)(2,1)S(1)}, bf16[1,16,4224]{2,1,0:T(8,128)(2,1)S(1)}, u32[]{:S(2)}, u32[]{:S(2)}) collective-permute-start(bf16[1,16,4224]{2,1,0:T(8,128)(2,1)S(1)} %bitcast.57), channel_id=1, source_target_pairs={{0,68},{1,69},{2,70},{3,71},{4,64},{5,65},{6,66},{7,67},{8,76},{9,... | collective-permute-start | bytes 405512 | tf_op jit(solution)/shard_map/ppermute | solution.py:40
  26.8 6.5 %collective-permute-start.4 = (bf16[2,1,16,4224]{3,2,1,0:T(8,128)(2,1)S(1)}, bf16[2,1,16,4224]{3,2,1,0:T(8,128)(2,1)S(1)}, u32[]{:S(2)}, u32[]{:S(2)}) collective-permute-start(bf16[2,1,16,4224]{3,2,1,0:T(8,128)(2,1)S(1)} %slice.24), channel_id=1, source_target_pairs={{0,1},{1,2},{2,3},{3,0},{4,5},{5,6},{6,7},{7,4},{8,9},{9,10},{10,1... | collective-permute-start | bytes 811016 | tf_op jit(solution)/shard_map/ppermute | solution.py:40
  27.2 7.7 %collective-permute-start.5 = (bf16[2,1,16,4224]{3,2,1,0:T(8,128)(2,1)S(1)}, bf16[2,1,16,4224]{3,2,1,0:T(8,128)(2,1)S(1)}, u32[]{:S(2)}, u32[]{:S(2)}) collective-permute-start(bf16[2,1,16,4224]{3,2,1,0:T(8,128)(2,1)S(1)} %slice.25), channel_id=1, source_target_pairs={{0,3},{1,0},{2,1},{3,2},{4,7},{5,4},{6,5},{7,6},{8,11},{9,8},{10,9... | collective-permute-start | bytes 811016 | tf_op jit(solution)/shard_map/ppermute | solution.py:40
  35.2 22.0 %collective-permute-start.12 = (bf16[256,4224]{1,0:T(8,128)(2,1)S(1)}, bf16[256,4224]{1,0:T(8,128)(2,1)S(1)}, u32[]{:S(2)}, u32[]{:S(2)}) collective-permute-start(bf16[256,4224]{1,0:T(8,128)(2,1)S(1)} %bitcast.40), channel_id=1, source_target_pairs={{0,32},{1,33},{2,34},{3,35},{4,36},{5,37},{6,38},{7,39},{8,40},{9,... | collective-permute-start | bytes 6488072 | tf_op jit(solution)/shard_map/ppermute | solution.py:40
  35.3 31.7 %collective-permute-start.7 = (bf16[256,4224]{1,0:T(8,128)(2,1)S(1)}, bf16[256,4224]{1,0:T(8,128)(2,1)S(1)}, u32[]{:S(2)}, u32[]{:S(2)}) collective-permute-start(bf16[256,4224]{1,0:T(8,128)(2,1)S(1)} %bitcast.41), channel_id=1, source_target_pairs={{0,24},{1,25},{2,26},{3,27},{4,28},{5,29},{6,30},{7,31},{8,0},{9,1... | collective-permute-start | bytes 6488072 | tf_op jit(solution)/shard_map/ppermute | solution.py:40
  38.4 32.3 %collective-permute-start.6 = (bf16[256,4224]{1,0:T(8,128)(2,1)S(1)}, bf16[256,4224]{1,0:T(8,128)(2,1)S(1)}, u32[]{:S(2)}, u32[]{:S(2)}) collective-permute-start(bf16[256,4224]{1,0:T(8,128)(2,1)S(1)} %bitcast.42), channel_id=1, source_target_pairs={{0,8},{1,9},{2,10},{3,11},{4,12},{5,13},{6,14},{7,15},{8,16},{9,17... | collective-permute-start | bytes 6488072 | tf_op jit(solution)/shard_map/ppermute | solution.py:40
  38.5 10.7 %collective-permute-start.8 = (bf16[1,2,16,4224]{3,2,1,0:T(8,128)(2,1)S(1)}, bf16[1,2,16,4224]{3,2,1,0:T(8,128)(2,1)S(1)}, u32[]{:S(2)}, u32[]{:S(2)}) collective-permute-start(bf16[1,2,16,4224]{3,2,1,0:T(8,128)(2,1)S(1)} %get-tuple-element.73), channel_id=1, source_target_pairs={{0,3},{1,0},{2,1},{3,2},{4,7},{5,4},{6,5},{7,6},{8,11},{9,8},{10,9... | collective-permute-start | bytes 811016 | tf_op jit(solution)/shard_map/ppermute | solution.py:40
  39.1 10.2 %collective-permute-start.9 = (bf16[1,2,16,4224]{3,2,1,0:T(8,128)(2,1)S(1)}, bf16[1,2,16,4224]{3,2,1,0:T(8,128)(2,1)S(1)}, u32[]{:S(2)}, u32[]{:S(2)}) collective-permute-start(bf16[1,2,16,4224]{3,2,1,0:T(8,128)(2,1)S(1)} %get-tuple-element.73), channel_id=1, source_target_pairs={{0,1},{1,2},{2,3},{3,0},{4,5},{5,6},{6,7},{7,4},{8,9},{9,10},{10,1... | collective-permute-start | bytes 811016 | tf_op jit(solution)/shard_map/ppermute | solution.py:40
  49.2 7.8 %collective-permute-start.11 = (bf16[1,1,16,4224]{3,2,1,0:T(8,128)(2,1)S(1)}, bf16[1,1,16,4224]{3,2,1,0:T(8,128)(2,1)S(1)}, u32[]{:S(2)}, u32[]{:S(2)}) collective-permute-start(bf16[1,1,16,4224]{3,2,1,0:T(8,128)(2,1)S(1)} %slice.33), channel_id=1, source_target_pairs={{0,3},{1,0},{2,1},{3,2},{4,7},{5,4},{6,5},{7,6},{8,11},{9,8},{10,9... | collective-permute-start | bytes 405512 | tf_op jit(solution)/shard_map/ppermute | solution.py:40
  49.3 7.7 %collective-permute-start.10 = (bf16[1,1,16,4224]{3,2,1,0:T(8,128)(2,1)S(1)}, bf16[1,1,16,4224]{3,2,1,0:T(8,128)(2,1)S(1)}, u32[]{:S(2)}, u32[]{:S(2)}) collective-permute-start(bf16[1,1,16,4224]{3,2,1,0:T(8,128)(2,1)S(1)} %slice.32), channel_id=1, source_target_pairs={{0,1},{1,2},{2,3},{3,0},{4,5},{5,6},{6,7},{7,4},{8,9},{9,10},{10,1... | collective-permute-start | bytes 405512 | tf_op jit(solution)/shard_map/ppermute | solution.py:40
  70.7 8.9 %collective-permute-start.13 = (bf16[256,4224]{1,0:T(8,128)(2,1)S(1)}, bf16[256,4224]{1,0:T(8,128)(2,1)S(1)}, u32[]{:S(2)}, u32[]{:S(2)}) collective-permute-start(bf16[256,4224]{1,0:T(8,128)(2,1)S(1)} %collective-permute-done.7.refs_0_.refs_13_), channel_id=1, source_target_pairs={{0,32},{1,33},{2,34},{3,35},{4,36},{5,37},{6,38},{7,39},{8,40},{9,... | collective-permute-start | bytes 6488072 | tf_op jit(solution)/shard_map/ppermute | solution.py:40
  70.7 8.9 %collective-permute-start.14 = (bf16[256,4224]{1,0:T(8,128)(2,1)S(1)}, bf16[256,4224]{1,0:T(8,128)(2,1)S(1)}, u32[]{:S(2)}, u32[]{:S(2)}) collective-permute-start(bf16[256,4224]{1,0:T(8,128)(2,1)S(1)} %collective-permute-done.6.refs_1_.refs_14_), channel_id=1, source_target_pairs={{0,32},{1,33},{2,34},{3,35},{4,36},{5,37},{6,38},{7,39},{8,40},{9,... | collective-permute-start | bytes 6488072 | tf_op jit(solution)/shard_map/ppermute | solution.py:40
  71.2 8.4 %collective-permute-start.15 = (bf16[128,4224]{1,0:T(8,128)(2,1)S(1)}, bf16[128,4224]{1,0:T(8,128)(2,1)S(1)}, u32[]{:S(2)}, u32[]{:S(2)}) collective-permute-start(bf16[128,4224]{1,0:T(8,128)(2,1)S(1)} %bitcast.45), channel_id=1, source_target_pairs={{0,32},{1,33},{2,34},{3,35},{4,36},{5,37},{6,38},{7,39},{8,40},{9,... | collective-permute-start | bytes 3244040 | tf_op jit(solution)/shard_map/ppermute | solution.py:40
  71.3 16.4 %collective-permute-start.20 = (bf16[128,4224]{1,0:T(8,128)(2,1)S(1)}, bf16[128,4224]{1,0:T(8,128)(2,1)S(1)}, u32[]{:S(2)}, u32[]{:S(2)}) collective-permute-start(bf16[128,4224]{1,0:T(8,128)(2,1)S(1)} %slice.30), channel_id=1, source_target_pairs={{0,8},{1,9},{2,10},{3,11},{4,12},{5,13},{6,14},{7,15},{8,16},{9,17... | collective-permute-start | bytes 3244040 | tf_op jit(solution)/shard_map/ppermute | solution.py:40
  71.5 16.3 %collective-permute-start.21 = (bf16[128,4224]{1,0:T(8,128)(2,1)S(1)}, bf16[128,4224]{1,0:T(8,128)(2,1)S(1)}, u32[]{:S(2)}, u32[]{:S(2)}) collective-permute-start(bf16[128,4224]{1,0:T(8,128)(2,1)S(1)} %slice.31), channel_id=1, source_target_pairs={{0,24},{1,25},{2,26},{3,27},{4,28},{5,29},{6,30},{7,31},{8,0},{9,1... | collective-permute-start | bytes 3244040 | tf_op jit(solution)/shard_map/ppermute | solution.py:40
  79.6 19.4 %collective-permute-start.17 = (bf16[128,4224]{1,0:T(8,128)(2,1)S(1)}, bf16[128,4224]{1,0:T(8,128)(2,1)S(1)}, u32[]{:S(2)}, u32[]{:S(2)}) collective-permute-start(bf16[128,4224]{1,0:T(8,128)(2,1)S(1)} %bitcast.46), channel_id=1, source_target_pairs={{0,24},{1,25},{2,26},{3,27},{4,28},{5,29},{6,30},{7,31},{8,0},{9,1... | collective-permute-start | bytes 3244040 | tf_op jit(solution)/shard_map/ppermute | solution.py:40
  79.8 19.5 %collective-permute-start.16 = (bf16[128,4224]{1,0:T(8,128)(2,1)S(1)}, bf16[128,4224]{1,0:T(8,128)(2,1)S(1)}, u32[]{:S(2)}, u32[]{:S(2)}) collective-permute-start(bf16[128,4224]{1,0:T(8,128)(2,1)S(1)} %bitcast.47), channel_id=1, source_target_pairs={{0,8},{1,9},{2,10},{3,11},{4,12},{5,13},{6,14},{7,15},{8,16},{9,17... | collective-permute-start | bytes 3244040 | tf_op jit(solution)/shard_map/ppermute | solution.py:40
  87.7 15.7 %collective-permute-start.22 = (bf16[128,4224]{1,0:T(8,128)(2,1)S(1)}, bf16[128,4224]{1,0:T(8,128)(2,1)S(1)}, u32[]{:S(2)}, u32[]{:S(2)}) collective-permute-start(bf16[128,4224]{1,0:T(8,128)(2,1)S(1)} %collective-permute-done.20.refs_0_.refs_19_), channel_id=1, source_target_pairs={{0,32},{1,33},{2,34},{3,35},{4,36},{5,37},{6,38},{7,39},{8,40},{9,... | collective-permute-start | bytes 3244040 | tf_op jit(solution)/shard_map/ppermute | solution.py:40
  87.8 15.7 %collective-permute-start.23 = (bf16[128,4224]{1,0:T(8,128)(2,1)S(1)}, bf16[128,4224]{1,0:T(8,128)(2,1)S(1)}, u32[]{:S(2)}, u32[]{:S(2)}) collective-permute-start(bf16[128,4224]{1,0:T(8,128)(2,1)S(1)} %collective-permute-done.21.refs_1_.refs_20_), channel_id=1, source_target_pairs={{0,32},{1,33},{2,34},{3,35},{4,36},{5,37},{6,38},{7,39},{8,40},{9,... | collective-permute-start | bytes 3244040 | tf_op jit(solution)/shard_map/ppermute | solution.py:40
  99.3 4.2 %collective-permute-start.25 = (bf16[128,4224]{1,0:T(8,128)(2,1)S(1)}, bf16[128,4224]{1,0:T(8,128)(2,1)S(1)}, u32[]{:S(2)}, u32[]{:S(2)}) collective-permute-start(bf16[128,4224]{1,0:T(8,128)(2,1)S(1)} %collective-permute-done.16.refs_3_.refs_22_), channel_id=1, source_target_pairs={{0,32},{1,33},{2,34},{3,35},{4,36},{5,37},{6,38},{7,39},{8,40},{9,... | collective-permute-start | bytes 3244040 | tf_op jit(solution)/shard_map/ppermute | solution.py:40
  99.3 4.3 %collective-permute-start.24 = (bf16[128,4224]{1,0:T(8,128)(2,1)S(1)}, bf16[128,4224]{1,0:T(8,128)(2,1)S(1)}, u32[]{:S(2)}, u32[]{:S(2)}) collective-permute-start(bf16[128,4224]{1,0:T(8,128)(2,1)S(1)} %collective-permute-done.17.refs_2_.refs_21_), channel_id=1, source_target_pairs={{0,32},{1,33},{2,34},{3,35},{4,36},{5,37},{6,38},{7,39},{8,40},{9,... | collective-permute-start | bytes 3244040 | tf_op jit(solution)/shard_map/ppermute | solution.py:40
  99.9 10.4 %collective-permute-start.19 = (bf16[64,4224]{1,0:T(8,128)(2,1)S(1)}, bf16[64,4224]{1,0:T(8,128)(2,1)S(1)}, u32[]{:S(2)}, u32[]{:S(2)}) collective-permute-start(bf16[64,4224]{1,0:T(8,128)(2,1)S(1)} %slice.29), channel_id=1, source_target_pairs={{0,24},{1,25},{2,26},{3,27},{4,28},{5,29},{6,30},{7,31},{8,0},{9,1... | collective-permute-start | bytes 1622024 | tf_op jit(solution)/shard_map/ppermute | solution.py:40
  103.5 10.6 %collective-permute-start.18 = (bf16[64,4224]{1,0:T(8,128)(2,1)S(1)}, bf16[64,4224]{1,0:T(8,128)(2,1)S(1)}, u32[]{:S(2)}, u32[]{:S(2)}) collective-permute-start(bf16[64,4224]{1,0:T(8,128)(2,1)S(1)} %slice.28), channel_id=1, source_target_pairs={{0,8},{1,9},{2,10},{3,11},{4,12},{5,13},{6,14},{7,15},{8,16},{9,17... | collective-permute-start | bytes 1622024 | tf_op jit(solution)/shard_map/ppermute | solution.py:40
  127.6 5.0 %collective-permute-start.30 = (f32[24,128]{1,0:T(8,128)S(1)}, f32[24,128]{1,0:T(8,128)S(1)}, u32[]{:S(2)}, u32[]{:S(2)}) collective-permute-start(f32[24,128]{1,0:T(8,128)S(1)} %log_add_fusion.5), channel_id=1, source_target_pairs={{0,68},{1,69},{2,70},{3,71},{4,64},{5,65},{6,66},{7,67},{8,76},{9,... | collective-permute-start | bytes 36872 | tf_op jit(solution)/shard_map/ppermute | solution.py:40
  136.6 5.0 %collective-permute-start.32 = (f32[24,128]{1,0:T(8,128)S(1)}, f32[24,128]{1,0:T(8,128)S(1)}, u32[]{:S(2)}, u32[]{:S(2)}) collective-permute-start(f32[24,128]{1,0:T(8,128)S(1)} %log_add_fusion.3), channel_id=1, source_target_pairs={{0,3},{1,2},{2,1},{3,0},{4,7},{5,6},{6,5},{7,4},{8,11},{9,10},{10,... | collective-permute-start | bytes 36872 | tf_op jit(solution)/shard_map/ppermute | solution.py:40
  145.4 5.0 %collective-permute-start.34 = (f32[24,128]{1,0:T(8,128)S(1)}, f32[24,128]{1,0:T(8,128)S(1)}, u32[]{:S(2)}, u32[]{:S(2)}) collective-permute-start(f32[24,128]{1,0:T(8,128)S(1)} %log_add_fusion.1), channel_id=1, source_target_pairs={{0,24},{1,25},{2,26},{3,27},{4,28},{5,29},{6,30},{7,31},{8,16},{9,... | collective-permute-start | bytes 36872 | tf_op jit(solution)/shard_map/ppermute | solution.py:40
  181.9 5.0 %collective-permute-start.37 = (f32[1,4096]{1,0:T(1,128)S(1)}, f32[1,4096]{1,0:T(1,128)S(1)}, u32[]{:S(2)}, u32[]{:S(2)}) collective-permute-start(f32[1,4096]{1,0:T(1,128)S(1)} %add.97), channel_id=1, source_target_pairs={{0,68},{1,69},{2,70},{3,71},{4,64},{5,65},{6,66},{7,67},{8,76},{9,... | collective-permute-start | bytes 49160 | tf_op jit(solution)/shard_map/ppermute | solution.py:40
  190.8 5.0 %collective-permute-start.39 = (f32[1,4096]{1,0:T(1,128)S(1)}, f32[1,4096]{1,0:T(1,128)S(1)}, u32[]{:S(2)}, u32[]{:S(2)}) collective-permute-start(f32[1,4096]{1,0:T(1,128)S(1)} %add.99), channel_id=1, source_target_pairs={{0,3},{1,2},{2,1},{3,0},{4,7},{5,6},{6,5},{7,4},{8,11},{9,10},{10,... | collective-permute-start | bytes 49160 | tf_op jit(solution)/shard_map/ppermute | solution.py:40
  199.7 5.0 %collective-permute-start.41 = (f32[1,4096]{1,0:T(1,128)S(1)}, f32[1,4096]{1,0:T(1,128)S(1)}, u32[]{:S(2)}, u32[]{:S(2)}) collective-permute-start(f32[1,4096]{1,0:T(1,128)S(1)} %add.101), channel_id=1, source_target_pairs={{0,24},{1,25},{2,26},{3,27},{4,28},{5,29},{6,30},{7,31},{8,16},{9,... | collective-permute-start | bytes 49160 | tf_op jit(solution)/shard_map/ppermute | solution.py:40
  (43 other events, 448.6 us)

commit v3 on v2

--- a/solution.py
+++ b/solution.py
@@ -78,12 +78,12 @@
     return jnp.stack([two, right, far, left], axis=1).reshape(groups * LANES, width)
 
 
-def normalize_kernel(place_ref, labels_ref, hidden_ref, gain_ref, *out_refs):
-    core = place_ref[0]
+def normalize_kernel(labels_ref, hidden_ref, gain_ref, *out_refs):
+    core = lax.axis_index("co")
     _, rows, features = hidden_ref.shape
     wide = hidden_ref[core].astype(jnp.float32)
     factor = lax.rsqrt(jnp.mean(wide * wide, axis=-1, keepdims=True) + EPS)
-    scaled = (wide * factor * gain_ref[...].astype(jnp.float32)).astype(jnp.bfloat16)
+    scaled = (wide * factor * gain_ref[...].astype(jnp.float32)[None]).astype(jnp.bfloat16)
     row = lax.broadcasted_iota(jnp.int32, (rows, LANES), 0)
     lane = lax.broadcasted_iota(jnp.int32, (rows, LANES), 1)
     label = jnp.zeros((rows, LANES), jnp.int32)
@@ -99,16 +99,16 @@
         at += out_ref.shape[0]
 
 
-def normalized(place, labels, hidden, gain):
+def normalized(labels, hidden, gain):
     _, _, features = hidden.shape
     smem, vmem = pl.BlockSpec(memory_space=pltpu.SMEM), pl.BlockSpec(memory_space=pltpu.VMEM)
     sets = pl.pallas_call(
         normalize_kernel,
         out_shape=[jax.ShapeDtypeStruct((groups * ROWS, features + LANES), jnp.bfloat16) for groups in SETS],
-        in_specs=[smem, smem, vmem, vmem],
+        in_specs=[smem, vmem, vmem],
         out_specs=[vmem] * len(SETS),
         name="normalized",
-    )(place, labels, hidden, gain[None])
+    )(labels, hidden, gain)
     return [rows.reshape(groups, ROWS, features + LANES) for rows, groups in zip(sets, SETS)]
 
 
@@ -351,7 +351,7 @@
     place = jnp.stack([core, lax.axis_index("y"), lax.axis_index("zh"), lax.axis_index("x")]).astype(jnp.int32)
     base = (lax.axis_index(VOCAB_FSDP) * columns).astype(jnp.int32).reshape(1)
     gain_wide = norm_gain.astype(jnp.float32)
-    own0, own1 = normalized(place, labels, hidden, norm_gain)
+    own0, own1 = normalized(labels, hidden, norm_gain)
     count = batches * own_rows * 32
     wt = head_weight.T
 

time: 206 us -> 206 us (level)
  waiting for transfers between devices: 103 us -> 100 us
  local copies, waits for them, and re-layouts: 12.5 us -> 15.3 us
    unnamed x67 -> x69, local copies, waits for them, and re-layouts: 10.9 us -> 15 us
    ppermute x42, waiting for transfers between devices: 103 us -> 100 us  [moved(): return lax.ppermute(value, AXES, pairs)]
  transfers between devices with their start and end apart: 42 -> 42, of which waited for: 33 -> 32; matrix products, arithmetic and copies ran while one was open for 3% -> 4% of each run, Pallas kernels for 7% -> 7%
where the time goes in v3:
time: 206 us
  waiting for transfers between devices  100 us (49%)
  Pallas kernels  44.2 us (21%)
  starting transfers between devices  40.4 us (20%)
  local copies, waits for them, and re-layouts  15.3 us (7%)
  other arithmetic  4.22 us (2%)
    ppermute x42, waiting for transfers between devices, moved(): return lax.ppermute(value, AXES, pairs)  100 us
    ppermute x42, starting transfers between devices, moved(): return lax.ppermute(value, AXES, pairs)  40.4 us
    pallas_call x1, Pallas kernels, backward(): pl.pallas_call(functools.partial(backward_kernel, sizes, widths, count),...  24.9 us
    pallas_call x4, Pallas kernels, forward(): pl.pallas_call(functools.partial(forward_kernel, features, sizes), out_sh...  15.2 us
    unnamed x69, local copies, waits for them, and re-layouts  15 us
  transfers between devices with their start and end apart: 42, of which 32 were waited for; matrix products, arithmetic and copies ran while one was open for 4% of the time, Pallas kernels for 7%

profile of v3, /device:TPU:6, one launch (start us, length us, event | category | flops | bytes accessed | tf_op | source)
XLA Modules:
  0.0 205.6 jit_solution(15331353401721130517)
XLA Ops:
  2.8 4.0 %collective-permute-start = (bf16[2,16,4224]{2,1,0:T(8,128)(2,1)}, bf16[2,16,4224]{2,1,0:T(8,128)(2,1)S(1)}, u32[]{:S(2)}, u32[]{:S(2)}) collective-permute-start(bf16[2,16,4224]{2,1,0:T(8,128)(2,1)} %bitcast.54), channel_id=1, source_target_pairs={{0,68},{1,69},{2,70},{3,71},{4,64},{5,65},{6,66},{7,67},{8,76},{9,... | collective-permute-start | bytes 811016 | tf_op jit(solution)/shard_map/ppermute | solution.py:40
  6.8 6.4 %copy.8 = bf16[4096,512]{0,1:T(8,128)(2,1)} copy(bf16[4096,512]{1,0:T(8,128)(2,1)} %param.9) | data formatting | bytes 8388608 | tf_op args[3]
  15.8 2.9 %collective-permute-start.3 = (bf16[1,16,4224]{2,1,0:T(8,128)(2,1)S(1)}, bf16[1,16,4224]{2,1,0:T(8,128)(2,1)S(1)}, u32[]{:S(2)}, u32[]{:S(2)}) collective-permute-start(bf16[1,16,4224]{2,1,0:T(8,128)(2,1)S(1)} %bitcast.57), channel_id=1, source_target_pairs={{0,68},{1,69},{2,70},{3,71},{4,64},{5,65},{6,66},{7,67},{8,76},{9,... | collective-permute-start | bytes 405512 | tf_op jit(solution)/shard_map/ppermute | solution.py:40
  18.7 3.9 %collective-permute-done.3 = bf16[1,16,4224]{2,1,0:T(8,128)(2,1)S(1)} collective-permute-done((bf16[1,16,4224]{2,1,0:T(8,128)(2,1)S(1)}, bf16[1,16,4224]{2,1,0:T(8,128)(2,1)S(1)}, u32[]{:S(2)}, u32[]{:S(2)}) %collective-permute-start.3) | collective-permute-done | bytes 135200 | tf_op jit(solution)/shard_map/ppermute | solution.py:40
  26.9 4.4 %collective-permute-done.4 = bf16[2,1,16,4224]{3,2,1,0:T(8,128)(2,1)S(1)} collective-permute-done((bf16[2,1,16,4224]{3,2,1,0:T(8,128)(2,1)S(1)}, bf16[2,1,16,4224]{3,2,1,0:T(8,128)(2,1)S(1)}, u32[]{:S(2)}, u32[]{:S(2)}) %collective-permute-start.4) | collective-permute-done | bytes 270368 | tf_op jit(solution)/shard_map/ppermute | solution.py:40
  33.4 3.1 %collective-permute-start.7 = (bf16[256,4224]{1,0:T(8,128)(2,1)S(1)}, bf16[256,4224]{1,0:T(8,128)(2,1)S(1)}, u32[]{:S(2)}, u32[]{:S(2)}) collective-permute-start(bf16[256,4224]{1,0:T(8,128)(2,1)S(1)} %bitcast.41), channel_id=1, source_target_pairs={{0,24},{1,25},{2,26},{3,27},{4,28},{5,29},{6,30},{7,31},{8,0},{9,1... | collective-permute-start | bytes 6488072 | tf_op jit(solution)/shard_map/ppermute | solution.py:40
  39.8 7.4 %collective-permute-done.8 = bf16[1,2,16,4224]{3,2,1,0:T(8,128)(2,1)S(1)} collective-permute-done((bf16[1,2,16,4224]{3,2,1,0:T(8,128)(2,1)S(1)}, bf16[1,2,16,4224]{3,2,1,0:T(8,128)(2,1)S(1)}, u32[]{:S(2)}, u32[]{:S(2)}) %collective-permute-start.8) | collective-permute-done | bytes 270368 | tf_op jit(solution)/shard_map/ppermute | solution.py:40
  47.3 3.3 %collective-permute-start.10 = (bf16[1,1,16,4224]{3,2,1,0:T(8,128)(2,1)S(1)}, bf16[1,1,16,4224]{3,2,1,0:T(8,128)(2,1)S(1)}, u32[]{:S(2)}, u32[]{:S(2)}) collective-permute-start(bf16[1,1,16,4224]{3,2,1,0:T(8,128)(2,1)S(1)} %slice.32), channel_id=1, source_target_pairs={{0,1},{1,2},{2,3},{3,0},{4,5},{5,6},{6,7},{7,4},{8,9},{9,10},{10,1... | collective-permute-start | bytes 405512 | tf_op jit(solution)/shard_map/ppermute | solution.py:40
  50.6 4.4 %collective-permute-done.11 = bf16[1,1,16,4224]{3,2,1,0:T(8,128)(2,1)S(1)} collective-permute-done((bf16[1,1,16,4224]{3,2,1,0:T(8,128)(2,1)S(1)}, bf16[1,1,16,4224]{3,2,1,0:T(8,128)(2,1)S(1)}, u32[]{:S(2)}, u32[]{:S(2)}) %collective-permute-start.11) | collective-permute-done | bytes 135200 | tf_op jit(solution)/shard_map/ppermute | solution.py:40
  59.4 5.6 %collective-permute-done.7.refs_0_.refs_13_ = bf16[256,4224]{1,0:T(8,128)(2,1)S(1)} collective-permute-done((bf16[256,4224]{1,0:T(8,128)(2,1)S(1)}, bf16[256,4224]{1,0:T(8,128)(2,1)S(1)}, u32[]{:S(2)}, u32[]{:S(2)}) %collective-permute-start.7) | collective-permute-done | bytes 2162720 | tf_op jit(solution)/shard_map/ppermute | solution.py:40
  65.0 3.7 %collective-permute-done.6.refs_1_.refs_14_ = bf16[256,4224]{1,0:T(8,128)(2,1)S(1)} collective-permute-done((bf16[256,4224]{1,0:T(8,128)(2,1)S(1)}, bf16[256,4224]{1,0:T(8,128)(2,1)S(1)}, u32[]{:S(2)}, u32[]{:S(2)}) %collective-permute-start.6) | collective-permute-done | bytes 2162720 | tf_op jit(solution)/shard_map/ppermute | solution.py:40
  69.5 3.3 %collective-permute-start.21 = (bf16[128,4224]{1,0:T(8,128)(2,1)S(1)}, bf16[128,4224]{1,0:T(8,128)(2,1)S(1)}, u32[]{:S(2)}, u32[]{:S(2)}) collective-permute-start(bf16[128,4224]{1,0:T(8,128)(2,1)S(1)} %slice.31), channel_id=1, source_target_pairs={{0,24},{1,25},{2,26},{3,27},{4,28},{5,29},{6,30},{7,31},{8,0},{9,1... | collective-permute-start | bytes 3244040 | tf_op jit(solution)/shard_map/ppermute | solution.py:40
  72.8 4.8 %collective-permute-done.15.refs_5_.refs_18_ = bf16[128,4224]{1,0:T(8,128)(2,1)S(1)} collective-permute-done((bf16[128,4224]{1,0:T(8,128)(2,1)S(1)}, bf16[128,4224]{1,0:T(8,128)(2,1)S(1)}, u32[]{:S(2)}, u32[]{:S(2)}) %collective-permute-start.15) | collective-permute-done | bytes 1081376 | tf_op jit(solution)/shard_map/ppermute | solution.py:40
  79.8 6.0 %collective-permute-done.20.refs_0_.refs_19_ = bf16[128,4224]{1,0:T(8,128)(2,1)S(1)} collective-permute-done((bf16[128,4224]{1,0:T(8,128)(2,1)S(1)}, bf16[128,4224]{1,0:T(8,128)(2,1)S(1)}, u32[]{:S(2)}, u32[]{:S(2)}) %collective-permute-start.20) | collective-permute-done | bytes 1081376 | tf_op jit(solution)/shard_map/ppermute | solution.py:40
  86.3 6.2 %forward.5 = (f32[512,1280]{1,0:T(8,128)S(1)}, f32[3,10,128]{2,1,0:T(8,128)S(1)}) custom-call(bf16[512,4096]{1,0:T(8,128)(2,1)S(1)} %bitcast.37, bf16[256,4224]{1,0:T(8,128)(2,1)S(1)} %collective-permute-done.7.refs_0_.refs_13_, bf16[256,4224]{1,0:T(8,128)(2,1)S(1)} %collective-permute-done.6.refs_1_.refs_14_, bf16[128,4224]{1,0:T(8,128)(2,1)S(1)} %bitcast.48, ...), custom_call_target="tpu_custom_call" | custom-call | flops 5368709120 | bytes 17629184 | tf_op jit(solution)/shard_map/forward/pallas_call | solution.py:159
  94.0 3.1 %collective-permute-done.17.refs_2_.refs_21_ = bf16[128,4224]{1,0:T(8,128)(2,1)S(1)} collective-permute-done((bf16[128,4224]{1,0:T(8,128)(2,1)S(1)}, bf16[128,4224]{1,0:T(8,128)(2,1)S(1)}, u32[]{:S(2)}, u32[]{:S(2)}) %collective-permute-start.17) | collective-permute-done | bytes 1081376 | tf_op jit(solution)/shard_map/ppermute | solution.py:40
  97.9 3.5 %collective-permute-start.19 = (bf16[64,4224]{1,0:T(8,128)(2,1)S(1)}, bf16[64,4224]{1,0:T(8,128)(2,1)S(1)}, u32[]{:S(2)}, u32[]{:S(2)}) collective-permute-start(bf16[64,4224]{1,0:T(8,128)(2,1)S(1)} %slice.29), channel_id=1, source_target_pairs={{0,24},{1,25},{2,26},{3,27},{4,28},{5,29},{6,30},{7,31},{8,0},{9,1... | collective-permute-start | bytes 1622024 | tf_op jit(solution)/shard_map/ppermute | solution.py:40
  101.6 5.0 %forward.6 = (f32[512,1024]{1,0:T(8,128)S(1)}, f32[3,8,128]{2,1,0:T(8,128)S(1)}) custom-call(bf16[512,4096]{1,0:T(8,128)(2,1)S(1)} %bitcast.38, bf16[128,4224]{1,0:T(8,128)(2,1)S(1)} %collective-permute-done.20.refs_0_.refs_19_, bf16[128,4224]{1,0:T(8,128)(2,1)S(1)} %collective-permute-done.21.refs_1_.refs_20_, ...), custom_call_target="tpu_custom_call" | custom-call | flops 4294967296 | bytes 14942208 | tf_op jit(solution)/shard_map/forward/pallas_call | solution.py:159
  108.6 3.5 %collective-permute-done.18.refs_0_.refs_27_ = bf16[64,4224]{1,0:T(8,128)(2,1)S(1)} collective-permute-done((bf16[64,4224]{1,0:T(8,128)(2,1)S(1)}, bf16[64,4224]{1,0:T(8,128)(2,1)S(1)}, u32[]{:S(2)}, u32[]{:S(2)}) %collective-permute-start.18) | collective-permute-done | bytes 540704 | tf_op jit(solution)/shard_map/ppermute | solution.py:40
  124.0 3.7 %collective-permute-done.29 = f32[24,128]{1,0:T(8,128)S(1)} collective-permute-done((f32[24,128]{1,0:T(8,128)S(1)}, f32[24,128]{1,0:T(8,128)S(1)}, u32[]{:S(2)}, u32[]{:S(2)}) %collective-permute-start.29) | collective-permute-done | bytes 12320 | tf_op jit(solution)/shard_map/ppermute | solution.py:40
  127.7 3.0 %collective-permute-start.30 = (f32[24,128]{1,0:T(8,128)S(1)}, f32[24,128]{1,0:T(8,128)S(1)}, u32[]{:S(2)}, u32[]{:S(2)}) collective-permute-start(f32[24,128]{1,0:T(8,128)S(1)} %log_add_fusion.5), channel_id=1, source_target_pairs={{0,68},{1,69},{2,70},{3,71},{4,64},{5,65},{6,66},{7,67},{8,76},{9,... | collective-permute-start | bytes 36872 | tf_op jit(solution)/shard_map/ppermute | solution.py:40
  133.6 3.2 %collective-permute-done.31 = f32[24,128]{1,0:T(8,128)S(1)} collective-permute-done((f32[24,128]{1,0:T(8,128)S(1)}, f32[24,128]{1,0:T(8,128)S(1)}, u32[]{:S(2)}, u32[]{:S(2)}) %collective-permute-start.31) | collective-permute-done | bytes 12320 | tf_op jit(solution)/shard_map/ppermute | solution.py:40
  137.1 4.6 %collective-permute-done.32 = f32[24,128]{1,0:T(8,128)S(1)} collective-permute-done((f32[24,128]{1,0:T(8,128)S(1)}, f32[24,128]{1,0:T(8,128)S(1)}, u32[]{:S(2)}, u32[]{:S(2)}) %collective-permute-start.32) | collective-permute-done | bytes 12320 | tf_op jit(solution)/shard_map/ppermute | solution.py:40
  141.8 3.7 %collective-permute-done.33 = f32[24,128]{1,0:T(8,128)S(1)} collective-permute-done((f32[24,128]{1,0:T(8,128)S(1)}, f32[24,128]{1,0:T(8,128)S(1)}, u32[]{:S(2)}, u32[]{:S(2)}) %collective-permute-start.33) | collective-permute-done | bytes 12320 | tf_op jit(solution)/shard_map/ppermute | solution.py:40
  145.7 4.8 %collective-permute-done.34 = f32[24,128]{1,0:T(8,128)S(1)} collective-permute-done((f32[24,128]{1,0:T(8,128)S(1)}, f32[24,128]{1,0:T(8,128)S(1)}, u32[]{:S(2)}, u32[]{:S(2)}) %collective-permute-start.34) | collective-permute-done | bytes 12320 | tf_op jit(solution)/shard_map/ppermute | solution.py:40
  151.2 24.9 %backward.1 = (f32[4096,512]{1,0:T(8,128)}, f32[1,4096]{1,0:T(1,128)}) custom-call(s32[4]{0:T(128)} %pad_add_fusion.place_ref, s32[1]{0:T(128)} %bitcast.4.base_ref, f32[3,4,128]{2,1,0:T(4,128)} %copy-done.15, f32[3,10,128]{2,1,0:T(8,128)} %copy-done.13, f32[3,8,128]{2,1,0:T(8,128)} %copy-done.14, f32[3,2,128]{2,1,0:T(2,128)} %copy-done.16, ...), custom_call_target="tpu_custom_call" | custom-call | flops 12884901888 | bytes 52428800 | tf_op jit(solution)/shard_map/backward/pallas_call | solution.py:308
  178.3 3.7 %collective-permute-done.36 = f32[1,4096]{1,0:T(1,128)S(1)} collective-permute-done((f32[1,4096]{1,0:T(1,128)S(1)}, f32[1,4096]{1,0:T(1,128)S(1)}, u32[]{:S(2)}, u32[]{:S(2)}) %collective-permute-start.36) | collective-permute-done | bytes 16416 | tf_op jit(solution)/shard_map/ppermute | solution.py:40
  182.1 3.0 %collective-permute-start.37 = (f32[1,4096]{1,0:T(1,128)S(1)}, f32[1,4096]{1,0:T(1,128)S(1)}, u32[]{:S(2)}, u32[]{:S(2)}) collective-permute-start(f32[1,4096]{1,0:T(1,128)S(1)} %add.97), channel_id=1, source_target_pairs={{0,68},{1,69},{2,70},{3,71},{4,64},{5,65},{6,66},{7,67},{8,76},{9,... | collective-permute-start | bytes 49160 | tf_op jit(solution)/shard_map/ppermute | solution.py:40
  187.2 3.7 %collective-permute-done.38 = f32[1,4096]{1,0:T(1,128)S(1)} collective-permute-done((f32[1,4096]{1,0:T(1,128)S(1)}, f32[1,4096]{1,0:T(1,128)S(1)}, u32[]{:S(2)}, u32[]{:S(2)}) %collective-permute-start.38) | collective-permute-done | bytes 16416 | tf_op jit(solution)/shard_map/ppermute | solution.py:40
  191.3 4.7 %collective-permute-done.39 = f32[1,4096]{1,0:T(1,128)S(1)} collective-permute-done((f32[1,4096]{1,0:T(1,128)S(1)}, f32[1,4096]{1,0:T(1,128)S(1)}, u32[]{:S(2)}, u32[]{:S(2)}) %collective-permute-start.39) | collective-permute-done | bytes 16416 | tf_op jit(solution)/shard_map/ppermute | solution.py:40
  196.1 3.7 %collective-permute-done.40 = f32[1,4096]{1,0:T(1,128)S(1)} collective-permute-done((f32[1,4096]{1,0:T(1,128)S(1)}, f32[1,4096]{1,0:T(1,128)S(1)}, u32[]{:S(2)}, u32[]{:S(2)}) %collective-permute-start.40) | collective-permute-done | bytes 16416 | tf_op jit(solution)/shard_map/ppermute | solution.py:40
  200.0 4.9 %collective-permute-done.41 = f32[1,4096]{1,0:T(1,128)S(1)} collective-permute-done((f32[1,4096]{1,0:T(1,128)S(1)}, f32[1,4096]{1,0:T(1,128)S(1)}, u32[]{:S(2)}, u32[]{:S(2)}) %collective-permute-start.41) | collective-permute-done | bytes 16416 | tf_op jit(solution)/shard_map/ppermute | solution.py:40
  (158 shorter events, 48.5 us)
Async XLA Ops:
  2.8 10.8 %collective-permute-start = (bf16[2,16,4224]{2,1,0:T(8,128)(2,1)}, bf16[2,16,4224]{2,1,0:T(8,128)(2,1)S(1)}, u32[]{:S(2)}, u32[]{:S(2)}) collective-permute-start(bf16[2,16,4224]{2,1,0:T(8,128)(2,1)} %bitcast.54), channel_id=1, source_target_pairs={{0,68},{1,69},{2,70},{3,71},{4,64},{5,65},{6,66},{7,67},{8,76},{9,... | collective-permute-start | bytes 811016 | tf_op jit(solution)/shard_map/ppermute | solution.py:40
  13.7 9.4 %collective-permute-start.1 = (bf16[2,2,16,4224]{3,2,1,0:T(8,128)(2,1)S(1)}, bf16[2,2,16,4224]{3,2,1,0:T(8,128)(2,1)S(1)}, u32[]{:S(2)}, u32[]{:S(2)}) collective-permute-start(bf16[2,2,16,4224]{3,2,1,0:T(8,128)(2,1)S(1)} %get-tuple-element.71), channel_id=1, source_target_pairs={{0,1},{1,2},{2,3},{3,0},{4,5},{5,6},{6,7},{7,4},{8,9},{9,10},{10,1... | collective-permute-start | bytes 1622024 | tf_op jit(solution)/shard_map/ppermute | solution.py:40
  14.2 10.6 %collective-permute-start.2 = (bf16[2,2,16,4224]{3,2,1,0:T(8,128)(2,1)S(1)}, bf16[2,2,16,4224]{3,2,1,0:T(8,128)(2,1)S(1)}, u32[]{:S(2)}, u32[]{:S(2)}) collective-permute-start(bf16[2,2,16,4224]{3,2,1,0:T(8,128)(2,1)S(1)} %get-tuple-element.71), channel_id=1, source_target_pairs={{0,3},{1,0},{2,1},{3,2},{4,7},{5,4},{6,5},{7,6},{8,11},{9,8},{10,9... | collective-permute-start | bytes 1622024 | tf_op jit(solution)/shard_map/ppermute | solution.py:40
  15.8 6.8 %collective-permute-start.3 = (bf16[1,16,4224]{2,1,0:T(8,128)(2,1)S(1)}, bf16[1,16,4224]{2,1,0:T(8,128)(2,1)S(1)}, u32[]{:S(2)}, u32[]{:S(2)}) collective-permute-start(bf16[1,16,4224]{2,1,0:T(8,128)(2,1)S(1)} %bitcast.57), channel_id=1, source_target_pairs={{0,68},{1,69},{2,70},{3,71},{4,64},{5,65},{6,66},{7,67},{8,76},{9,... | collective-permute-start | bytes 405512 | tf_op jit(solution)/shard_map/ppermute | solution.py:40
  24.8 6.5 %collective-permute-start.4 = (bf16[2,1,16,4224]{3,2,1,0:T(8,128)(2,1)S(1)}, bf16[2,1,16,4224]{3,2,1,0:T(8,128)(2,1)S(1)}, u32[]{:S(2)}, u32[]{:S(2)}) collective-permute-start(bf16[2,1,16,4224]{3,2,1,0:T(8,128)(2,1)S(1)} %slice.24), channel_id=1, source_target_pairs={{0,1},{1,2},{2,3},{3,0},{4,5},{5,6},{6,7},{7,4},{8,9},{9,10},{10,1... | collective-permute-start | bytes 811016 | tf_op jit(solution)/shard_map/ppermute | solution.py:40
  25.2 7.7 %collective-permute-start.5 = (bf16[2,1,16,4224]{3,2,1,0:T(8,128)(2,1)S(1)}, bf16[2,1,16,4224]{3,2,1,0:T(8,128)(2,1)S(1)}, u32[]{:S(2)}, u32[]{:S(2)}) collective-permute-start(bf16[2,1,16,4224]{3,2,1,0:T(8,128)(2,1)S(1)} %slice.25), channel_id=1, source_target_pairs={{0,3},{1,0},{2,1},{3,2},{4,7},{5,4},{6,5},{7,6},{8,11},{9,8},{10,9... | collective-permute-start | bytes 811016 | tf_op jit(solution)/shard_map/ppermute | solution.py:40
  33.3 22.0 %collective-permute-start.12 = (bf16[256,4224]{1,0:T(8,128)(2,1)S(1)}, bf16[256,4224]{1,0:T(8,128)(2,1)S(1)}, u32[]{:S(2)}, u32[]{:S(2)}) collective-permute-start(bf16[256,4224]{1,0:T(8,128)(2,1)S(1)} %bitcast.40), channel_id=1, source_target_pairs={{0,32},{1,33},{2,34},{3,35},{4,36},{5,37},{6,38},{7,39},{8,40},{9,... | collective-permute-start | bytes 6488072 | tf_op jit(solution)/shard_map/ppermute | solution.py:40
  33.4 31.7 %collective-permute-start.7 = (bf16[256,4224]{1,0:T(8,128)(2,1)S(1)}, bf16[256,4224]{1,0:T(8,128)(2,1)S(1)}, u32[]{:S(2)}, u32[]{:S(2)}) collective-permute-start(bf16[256,4224]{1,0:T(8,128)(2,1)S(1)} %bitcast.41), channel_id=1, source_target_pairs={{0,24},{1,25},{2,26},{3,27},{4,28},{5,29},{6,30},{7,31},{8,0},{9,1... | collective-permute-start | bytes 6488072 | tf_op jit(solution)/shard_map/ppermute | solution.py:40
  36.4 32.3 %collective-permute-start.6 = (bf16[256,4224]{1,0:T(8,128)(2,1)S(1)}, bf16[256,4224]{1,0:T(8,128)(2,1)S(1)}, u32[]{:S(2)}, u32[]{:S(2)}) collective-permute-start(bf16[256,4224]{1,0:T(8,128)(2,1)S(1)} %bitcast.42), channel_id=1, source_target_pairs={{0,8},{1,9},{2,10},{3,11},{4,12},{5,13},{6,14},{7,15},{8,16},{9,17... | collective-permute-start | bytes 6488072 | tf_op jit(solution)/shard_map/ppermute | solution.py:40
  36.5 10.7 %collective-permute-start.8 = (bf16[1,2,16,4224]{3,2,1,0:T(8,128)(2,1)S(1)}, bf16[1,2,16,4224]{3,2,1,0:T(8,128)(2,1)S(1)}, u32[]{:S(2)}, u32[]{:S(2)}) collective-permute-start(bf16[1,2,16,4224]{3,2,1,0:T(8,128)(2,1)S(1)} %get-tuple-element.73), channel_id=1, source_target_pairs={{0,3},{1,0},{2,1},{3,2},{4,7},{5,4},{6,5},{7,6},{8,11},{9,8},{10,9... | collective-permute-start | bytes 811016 | tf_op jit(solution)/shard_map/ppermute | solution.py:40
  37.1 10.2 %collective-permute-start.9 = (bf16[1,2,16,4224]{3,2,1,0:T(8,128)(2,1)S(1)}, bf16[1,2,16,4224]{3,2,1,0:T(8,128)(2,1)S(1)}, u32[]{:S(2)}, u32[]{:S(2)}) collective-permute-start(bf16[1,2,16,4224]{3,2,1,0:T(8,128)(2,1)S(1)} %get-tuple-element.73), channel_id=1, source_target_pairs={{0,1},{1,2},{2,3},{3,0},{4,5},{5,6},{6,7},{7,4},{8,9},{9,10},{10,1... | collective-permute-start | bytes 811016 | tf_op jit(solution)/shard_map/ppermute | solution.py:40
  47.2 7.8 %collective-permute-start.11 = (bf16[1,1,16,4224]{3,2,1,0:T(8,128)(2,1)S(1)}, bf16[1,1,16,4224]{3,2,1,0:T(8,128)(2,1)S(1)}, u32[]{:S(2)}, u32[]{:S(2)}) collective-permute-start(bf16[1,1,16,4224]{3,2,1,0:T(8,128)(2,1)S(1)} %slice.33), channel_id=1, source_target_pairs={{0,3},{1,0},{2,1},{3,2},{4,7},{5,4},{6,5},{7,6},{8,11},{9,8},{10,9... | collective-permute-start | bytes 405512 | tf_op jit(solution)/shard_map/ppermute | solution.py:40
  47.3 7.7 %collective-permute-start.10 = (bf16[1,1,16,4224]{3,2,1,0:T(8,128)(2,1)S(1)}, bf16[1,1,16,4224]{3,2,1,0:T(8,128)(2,1)S(1)}, u32[]{:S(2)}, u32[]{:S(2)}) collective-permute-start(bf16[1,1,16,4224]{3,2,1,0:T(8,128)(2,1)S(1)} %slice.32), channel_id=1, source_target_pairs={{0,1},{1,2},{2,3},{3,0},{4,5},{5,6},{6,7},{7,4},{8,9},{9,10},{10,1... | collective-permute-start | bytes 405512 | tf_op jit(solution)/shard_map/ppermute | solution.py:40
  68.7 8.9 %collective-permute-start.13 = (bf16[256,4224]{1,0:T(8,128)(2,1)S(1)}, bf16[256,4224]{1,0:T(8,128)(2,1)S(1)}, u32[]{:S(2)}, u32[]{:S(2)}) collective-permute-start(bf16[256,4224]{1,0:T(8,128)(2,1)S(1)} %collective-permute-done.7.refs_0_.refs_13_), channel_id=1, source_target_pairs={{0,32},{1,33},{2,34},{3,35},{4,36},{5,37},{6,38},{7,39},{8,40},{9,... | collective-permute-start | bytes 6488072 | tf_op jit(solution)/shard_map/ppermute | solution.py:40
  68.7 8.9 %collective-permute-start.14 = (bf16[256,4224]{1,0:T(8,128)(2,1)S(1)}, bf16[256,4224]{1,0:T(8,128)(2,1)S(1)}, u32[]{:S(2)}, u32[]{:S(2)}) collective-permute-start(bf16[256,4224]{1,0:T(8,128)(2,1)S(1)} %collective-permute-done.6.refs_1_.refs_14_), channel_id=1, source_target_pairs={{0,32},{1,33},{2,34},{3,35},{4,36},{5,37},{6,38},{7,39},{8,40},{9,... | collective-permute-start | bytes 6488072 | tf_op jit(solution)/shard_map/ppermute | solution.py:40
  69.3 8.4 %collective-permute-start.15 = (bf16[128,4224]{1,0:T(8,128)(2,1)S(1)}, bf16[128,4224]{1,0:T(8,128)(2,1)S(1)}, u32[]{:S(2)}, u32[]{:S(2)}) collective-permute-start(bf16[128,4224]{1,0:T(8,128)(2,1)S(1)} %bitcast.45), channel_id=1, source_target_pairs={{0,32},{1,33},{2,34},{3,35},{4,36},{5,37},{6,38},{7,39},{8,40},{9,... | collective-permute-start | bytes 3244040 | tf_op jit(solution)/shard_map/ppermute | solution.py:40
  69.3 16.4 %collective-permute-start.20 = (bf16[128,4224]{1,0:T(8,128)(2,1)S(1)}, bf16[128,4224]{1,0:T(8,128)(2,1)S(1)}, u32[]{:S(2)}, u32[]{:S(2)}) collective-permute-start(bf16[128,4224]{1,0:T(8,128)(2,1)S(1)} %slice.30), channel_id=1, source_target_pairs={{0,8},{1,9},{2,10},{3,11},{4,12},{5,13},{6,14},{7,15},{8,16},{9,17... | collective-permute-start | bytes 3244040 | tf_op jit(solution)/shard_map/ppermute | solution.py:40
  69.5 16.3 %collective-permute-start.21 = (bf16[128,4224]{1,0:T(8,128)(2,1)S(1)}, bf16[128,4224]{1,0:T(8,128)(2,1)S(1)}, u32[]{:S(2)}, u32[]{:S(2)}) collective-permute-start(bf16[128,4224]{1,0:T(8,128)(2,1)S(1)} %slice.31), channel_id=1, source_target_pairs={{0,24},{1,25},{2,26},{3,27},{4,28},{5,29},{6,30},{7,31},{8,0},{9,1... | collective-permute-start | bytes 3244040 | tf_op jit(solution)/shard_map/ppermute | solution.py:40
  77.7 19.4 %collective-permute-start.17 = (bf16[128,4224]{1,0:T(8,128)(2,1)S(1)}, bf16[128,4224]{1,0:T(8,128)(2,1)S(1)}, u32[]{:S(2)}, u32[]{:S(2)}) collective-permute-start(bf16[128,4224]{1,0:T(8,128)(2,1)S(1)} %bitcast.46), channel_id=1, source_target_pairs={{0,24},{1,25},{2,26},{3,27},{4,28},{5,29},{6,30},{7,31},{8,0},{9,1... | collective-permute-start | bytes 3244040 | tf_op jit(solution)/shard_map/ppermute | solution.py:40
  77.8 19.5 %collective-permute-start.16 = (bf16[128,4224]{1,0:T(8,128)(2,1)S(1)}, bf16[128,4224]{1,0:T(8,128)(2,1)S(1)}, u32[]{:S(2)}, u32[]{:S(2)}) collective-permute-start(bf16[128,4224]{1,0:T(8,128)(2,1)S(1)} %bitcast.47), channel_id=1, source_target_pairs={{0,8},{1,9},{2,10},{3,11},{4,12},{5,13},{6,14},{7,15},{8,16},{9,17... | collective-permute-start | bytes 3244040 | tf_op jit(solution)/shard_map/ppermute | solution.py:40
  85.8 15.7 %collective-permute-start.22 = (bf16[128,4224]{1,0:T(8,128)(2,1)S(1)}, bf16[128,4224]{1,0:T(8,128)(2,1)S(1)}, u32[]{:S(2)}, u32[]{:S(2)}) collective-permute-start(bf16[128,4224]{1,0:T(8,128)(2,1)S(1)} %collective-permute-done.20.refs_0_.refs_19_), channel_id=1, source_target_pairs={{0,32},{1,33},{2,34},{3,35},{4,36},{5,37},{6,38},{7,39},{8,40},{9,... | collective-permute-start | bytes 3244040 | tf_op jit(solution)/shard_map/ppermute | solution.py:40
  85.8 15.7 %collective-permute-start.23 = (bf16[128,4224]{1,0:T(8,128)(2,1)S(1)}, bf16[128,4224]{1,0:T(8,128)(2,1)S(1)}, u32[]{:S(2)}, u32[]{:S(2)}) collective-permute-start(bf16[128,4224]{1,0:T(8,128)(2,1)S(1)} %collective-permute-done.21.refs_1_.refs_20_), channel_id=1, source_target_pairs={{0,32},{1,33},{2,34},{3,35},{4,36},{5,37},{6,38},{7,39},{8,40},{9,... | collective-permute-start | bytes 3244040 | tf_op jit(solution)/shard_map/ppermute | solution.py:40
  97.4 4.2 %collective-permute-start.25 = (bf16[128,4224]{1,0:T(8,128)(2,1)S(1)}, bf16[128,4224]{1,0:T(8,128)(2,1)S(1)}, u32[]{:S(2)}, u32[]{:S(2)}) collective-permute-start(bf16[128,4224]{1,0:T(8,128)(2,1)S(1)} %collective-permute-done.16.refs_3_.refs_22_), channel_id=1, source_target_pairs={{0,32},{1,33},{2,34},{3,35},{4,36},{5,37},{6,38},{7,39},{8,40},{9,... | collective-permute-start | bytes 3244040 | tf_op jit(solution)/shard_map/ppermute | solution.py:40
  97.4 4.3 %collective-permute-start.24 = (bf16[128,4224]{1,0:T(8,128)(2,1)S(1)}, bf16[128,4224]{1,0:T(8,128)(2,1)S(1)}, u32[]{:S(2)}, u32[]{:S(2)}) collective-permute-start(bf16[128,4224]{1,0:T(8,128)(2,1)S(1)} %collective-permute-done.17.refs_2_.refs_21_), channel_id=1, source_target_pairs={{0,32},{1,33},{2,34},{3,35},{4,36},{5,37},{6,38},{7,39},{8,40},{9,... | collective-permute-start | bytes 3244040 | tf_op jit(solution)/shard_map/ppermute | solution.py:40
  97.9 10.6 %collective-permute-start.19 = (bf16[64,4224]{1,0:T(8,128)(2,1)S(1)}, bf16[64,4224]{1,0:T(8,128)(2,1)S(1)}, u32[]{:S(2)}, u32[]{:S(2)}) collective-permute-start(bf16[64,4224]{1,0:T(8,128)(2,1)S(1)} %slice.29), channel_id=1, source_target_pairs={{0,24},{1,25},{2,26},{3,27},{4,28},{5,29},{6,30},{7,31},{8,0},{9,1... | collective-permute-start | bytes 1622024 | tf_op jit(solution)/shard_map/ppermute | solution.py:40
  101.5 10.6 %collective-permute-start.18 = (bf16[64,4224]{1,0:T(8,128)(2,1)S(1)}, bf16[64,4224]{1,0:T(8,128)(2,1)S(1)}, u32[]{:S(2)}, u32[]{:S(2)}) collective-permute-start(bf16[64,4224]{1,0:T(8,128)(2,1)S(1)} %slice.28), channel_id=1, source_target_pairs={{0,8},{1,9},{2,10},{3,11},{4,12},{5,13},{6,14},{7,15},{8,16},{9,17... | collective-permute-start | bytes 1622024 | tf_op jit(solution)/shard_map/ppermute | solution.py:40
  127.7 5.0 %collective-permute-start.30 = (f32[24,128]{1,0:T(8,128)S(1)}, f32[24,128]{1,0:T(8,128)S(1)}, u32[]{:S(2)}, u32[]{:S(2)}) collective-permute-start(f32[24,128]{1,0:T(8,128)S(1)} %log_add_fusion.5), channel_id=1, source_target_pairs={{0,68},{1,69},{2,70},{3,71},{4,64},{5,65},{6,66},{7,67},{8,76},{9,... | collective-permute-start | bytes 36872 | tf_op jit(solution)/shard_map/ppermute | solution.py:40
  136.7 5.0 %collective-permute-start.32 = (f32[24,128]{1,0:T(8,128)S(1)}, f32[24,128]{1,0:T(8,128)S(1)}, u32[]{:S(2)}, u32[]{:S(2)}) collective-permute-start(f32[24,128]{1,0:T(8,128)S(1)} %log_add_fusion.3), channel_id=1, source_target_pairs={{0,3},{1,2},{2,1},{3,0},{4,7},{5,6},{6,5},{7,4},{8,11},{9,10},{10,... | collective-permute-start | bytes 36872 | tf_op jit(solution)/shard_map/ppermute | solution.py:40
  145.5 5.0 %collective-permute-start.34 = (f32[24,128]{1,0:T(8,128)S(1)}, f32[24,128]{1,0:T(8,128)S(1)}, u32[]{:S(2)}, u32[]{:S(2)}) collective-permute-start(f32[24,128]{1,0:T(8,128)S(1)} %log_add_fusion.1), channel_id=1, source_target_pairs={{0,24},{1,25},{2,26},{3,27},{4,28},{5,29},{6,30},{7,31},{8,16},{9,... | collective-permute-start | bytes 36872 | tf_op jit(solution)/shard_map/ppermute | solution.py:40
  182.1 5.0 %collective-permute-start.37 = (f32[1,4096]{1,0:T(1,128)S(1)}, f32[1,4096]{1,0:T(1,128)S(1)}, u32[]{:S(2)}, u32[]{:S(2)}) collective-permute-start(f32[1,4096]{1,0:T(1,128)S(1)} %add.97), channel_id=1, source_target_pairs={{0,68},{1,69},{2,70},{3,71},{4,64},{5,65},{6,66},{7,67},{8,76},{9,... | collective-permute-start | bytes 49160 | tf_op jit(solution)/shard_map/ppermute | solution.py:40
  191.0 5.0 %collective-permute-start.39 = (f32[1,4096]{1,0:T(1,128)S(1)}, f32[1,4096]{1,0:T(1,128)S(1)}, u32[]{:S(2)}, u32[]{:S(2)}) collective-permute-start(f32[1,4096]{1,0:T(1,128)S(1)} %add.99), channel_id=1, source_target_pairs={{0,3},{1,2},{2,1},{3,0},{4,7},{5,6},{6,5},{7,4},{8,11},{9,10},{10,... | collective-permute-start | bytes 49160 | tf_op jit(solution)/shard_map/ppermute | solution.py:40
  199.9 5.0 %collective-permute-start.41 = (f32[1,4096]{1,0:T(1,128)S(1)}, f32[1,4096]{1,0:T(1,128)S(1)}, u32[]{:S(2)}, u32[]{:S(2)}) collective-permute-start(f32[1,4096]{1,0:T(1,128)S(1)} %add.101), channel_id=1, source_target_pairs={{0,24},{1,25},{2,26},{3,27},{4,28},{5,29},{6,30},{7,31},{8,16},{9,... | collective-permute-start | bytes 49160 | tf_op jit(solution)/shard_map/ppermute | solution.py:40
  (44 other events, 439.8 us)
